TPU v7x, 512 devices: a whole 4x8x8 slice. The times are simulated.
512 devices in a mesh: dp: 32 (over x, y_hi, core), expert: 16 (over y_lo, z).
Axes of the slice: x: 4, y: 8 (y_hi: 4, y_lo: 2; y = y_hi * 2 + y_lo), z: 8, core: 2. Of those that a mesh axis runs over, the one named last changes fastest.
Arguments:
- tokens: bfloat16 [1024, 8192], P('expert', 'dp'), may hold values from -6 to 6
- gate_up: bfloat16 [16, 8192, 3584], P('expert', 'dp'), may hold values from -0.0625 to 0.0625
- down: bfloat16 [16, 1792, 8192], P('expert', None, 'dp'), may hold values from -0.125 to 0.125
- expert_ids: int32 [1024, 2], P('expert'), may hold values from 0 to 15, all different within a row; in each aligned block of 64 rows (0 to 63, 64 to 127, ...) at most 12 rows name the same one
- gate_values: float32 [1024, 2], P('expert'), may hold values from 0.1 to 0.6
- out_grad: bfloat16 [1024, 8192], P('expert', 'dp'), may hold values from -1.5 to 1.5
Outputs:
- moe_out: bfloat16 [1024, 8192], P('expert', 'dp')
- token_grad: bfloat16 [1024, 8192], P('expert', 'dp')
Inputs may be any that keep to these rules, and one draw needn't show every extreme that they name: `expert_ids`: each row names 2 different experts. Among the 64 rows of one device no expert is named more than 12 times, and in some device's rows one expert is named exactly 12 times.
All inputs are finite; a program needn't handle non-finite values.
Results may differ from a plain program's by a relative error of at most 0.0065.
Values may be sent and summed in bfloat16 or wider, within the bound.
No kernel may reach another device: no remote copies, remote signals or barrier semaphores. Data moves between devices by JAX's collectives and lax.ppermute only.
A program may use at most 64 MiB of HBM per device.

v0:
```python
import jax
import jax.numpy as jnp
from jax import lax
from jax.sharding import PartitionSpec as P


def swap_blocks(blocks):
    return lax.all_to_all(blocks, "expert", split_axis=0, concat_axis=0, tiled=True)


def activate(projected, hidden_units):
    gate_pre = projected[:, :hidden_units]
    up_pre = projected[:, hidden_units:]
    sigmoid_gate = jax.nn.sigmoid(gate_pre)
    return (gate_pre * sigmoid_gate * up_pre).astype(jnp.bfloat16)


def backward_act(hidden_grad, projected, hidden_units):
    gate_pre = projected[:, :hidden_units]
    up_pre = projected[:, hidden_units:]
    sigmoid_gate = jax.nn.sigmoid(gate_pre)
    gate_grad = hidden_grad * up_pre * sigmoid_gate * (1.0 + gate_pre * (1.0 - sigmoid_gate))
    up_grad = hidden_grad * gate_pre * sigmoid_gate
    return jnp.concatenate([gate_grad, up_grad], axis=1).astype(jnp.bfloat16)


def local(tokens, gate_up, down, expert_ids, gate_values, out_grad):
    tok_count, width_part = tokens.shape
    top_count = expert_ids.shape[1]
    expert_count = lax.axis_size("expert")
    capacity = tok_count * top_count * 3 // (2 * expert_count)
    slot_total = expert_count * capacity
    share_rows = slot_total // lax.axis_size("dp")
    hidden_units = down.shape[1]
    w_gate_up = gate_up[0]
    w_down = down[0]
    flat_ids = expert_ids.reshape(-1)
    onehot = (flat_ids[:, None] == jnp.arange(expert_count, dtype=jnp.int32)).astype(jnp.int32)
    slot_rank = jnp.sum((jnp.cumsum(onehot, axis=0) - 1) * onehot, axis=1)
    places = flat_ids * capacity + slot_rank
    select = (places[:, None] == jnp.arange(slot_total, dtype=jnp.int32)).astype(jnp.bfloat16)
    token_select = jnp.sum(select.reshape(tok_count, top_count, slot_total), axis=1)

    def place_rows(selector, values):
        placed = lax.dot_general(
            selector, values, (((0,), (0,)), ((), ())), preferred_element_type=jnp.float32
        )
        return placed.astype(jnp.bfloat16).reshape(expert_count, capacity, width_part)

    scaled = (gate_values[:, :, None] * out_grad[:, None, :].astype(jnp.float32)).astype(
        jnp.bfloat16
    )
    token_send = place_rows(token_select, tokens)
    grad_send = place_rows(select, scaled.reshape(tok_count * top_count, width_part))
    arrived = swap_blocks(token_send)
    token_slots = arrived.reshape(slot_total, width_part)
    projected_all = lax.psum(
        jnp.dot(token_slots, w_gate_up, preferred_element_type=jnp.float32), "dp"
    )
    hidden = activate(projected_all, hidden_units)
    outputs = jnp.dot(hidden, w_down, preferred_element_type=jnp.float32).astype(jnp.bfloat16)
    projected = lax.dynamic_slice_in_dim(
        projected_all, lax.axis_index("dp") * share_rows, share_rows, 0
    )
    returned = swap_blocks(outputs.reshape(expert_count, capacity, width_part)).reshape(
        slot_total, width_part
    )
    picked = jnp.take(returned, places, axis=0).reshape(tok_count, top_count, width_part)
    moe_out = jnp.sum(gate_values[:, :, None] * picked.astype(jnp.float32), axis=1).astype(
        jnp.bfloat16
    )
    grad_arrived = swap_blocks(grad_send)
    grad_slots = grad_arrived.reshape(slot_total, width_part)
    hidden_grad = lax.psum_scatter(
        lax.dot_general(
            grad_slots, w_down, (((1,), (1,)), ((), ())), preferred_element_type=jnp.float32
        ),
        "dp",
        scatter_dimension=0,
        tiled=True,
    )
    pre_grad = backward_act(hidden_grad, projected, hidden_units)
    product = lax.dot_general(
        lax.all_gather(pre_grad, "dp", axis=0, tiled=True),
        w_gate_up,
        (((1,), (1,)), ((), ())),
        preferred_element_type=jnp.float32,
    )
    input_grad = product.astype(jnp.bfloat16)
    grad_back = swap_blocks(input_grad.reshape(expert_count, capacity, width_part)).reshape(
        slot_total, width_part
    )
    grad_picked = jnp.take(grad_back, places, axis=0).reshape(tok_count, top_count, width_part)
    token_grad = jnp.sum(grad_picked.astype(jnp.float32), axis=1).astype(jnp.bfloat16)
    return (moe_out, token_grad)


def solution(mesh):
    return jax.shard_map(
        local,
        mesh=mesh,
        in_specs=(
            P("expert", "dp"),
            P("expert", "dp", None),
            P("expert", None, "dp"),
            P("expert", None),
            P("expert", None),
            P("expert", "dp"),
        ),
        out_specs=(P("expert", "dp"), P("expert", "dp")),
        check_vma=False,
    )
```

profile of v0, /device:TPU:8, one launch (start us, length us, event | category | flops | bytes accessed | tf_op | source)
XLA Modules:
  0.0 419.7 jit_solution(1335757634219932121)
XLA Ops:
  9.7 1.0 convolution_convert_fusion.2
  10.7 18.9 %all_to_all.20 = bf16[16,12,256]{2,1,0:T(8,128)(2,1)S(1)} all-to-all(bf16[16,12,256]{2,1,0:T(8,128)(2,1)S(1)} %reshape.65), channel_id=1, replica_groups=mesh['dp'=32,'expert'=16] {'expert'}, dimensions={0} | all-to-all | bytes 196608 | tf_op jit(solution)/shard_map/all_to_all | solution.py:8
  29.7 2.1 fusion.3
  33.2 11.6 %all_to_all.21 = bf16[16,12,256]{2,1,0:T(8,128)(2,1)S(1)} all-to-all(bf16[16,12,256]{2,1,0:T(8,128)(2,1)S(1)} %reshape.69), channel_id=1, replica_groups=mesh['dp'=32,'expert'=16] {'expert'}, dimensions={0} | all-to-all | bytes 196608 | tf_op jit(solution)/shard_map/all_to_all | solution.py:8
  44.9 1.6 fusion.9
  46.5 88.8 %fusion = f32[8,1792]{1,0:T(8,128)S(1)} fusion(f32[192,1792]{1,0:T(8,128)S(1)} %fusion.9), kind=kCustom, calls=%all-reduce-scatter | all-reduce-scatter fusion | flops 458753 | bytes 1435648
  135.4 1.3 collective-permute-start.6
  136.7 1.3 collective-permute-start.5
  138.0 1.3 collective-permute-start.7
  139.3 1.3 collective-permute-start.4
  140.6 6.9 %collective-permute-start.3 = (f32[8,1792]{1,0:T(8,128)S(1)}, f32[8,1792]{1,0:T(8,128)S(1)}, u32[]{:S(2)}, u32[]{:S(2)}) collective-permute-start(f32[8,1792]{1,0:T(8,128)S(1)} %fusion), channel_id=1, source_target_pairs={{0,64},{16,80},{32,96},{48,112},{64,128},{80,144},{96,160},{112,17... | collective-permute-start | bytes 172040
  147.5 1.3 collective-permute-start.2
  148.8 7.0 %collective-permute-start.1 = (f32[8,1792]{1,0:T(8,128)S(1)}, f32[8,1792]{1,0:T(8,128)S(1)}, u32[]{:S(2)}, u32[]{:S(2)}) collective-permute-start(f32[8,1792]{1,0:T(8,128)S(1)} %fusion), channel_id=1, source_target_pairs={{0,32},{16,48},{32,64},{48,80},{64,96},{80,112},{96,128},{112,144}... | collective-permute-start | bytes 172040
  155.8 3.8 collective-permute-start
  159.6 1.3 dynamic-slice.6
  161.6 1.0 concatenate.5
  162.6 170.5 %all-reduce.4.cloned.1.call-done = f32[192,3584]{1,0:T(8,128)} async-done(((f32[192,3584]{1,0:T(8,128)}), f32[192,3584]{1,0:T(8,128)}) %all-reduce.4.cloned.1.call-update) | async-done | bytes 2752528 | tf_op jit(solution)/shard_map/psum | solution.py:57
  333.1 1.0 fusion.20
  334.8 2.5 convolution_convert_fusion.1
  338.0 9.0 %all-to-all-start.1 = ((bf16[16,12,256]{2,1,0:T(8,128)(2,1)}), bf16[16,12,256]{2,1,0:T(8,128)(2,1)S(1)}, u32[]{:S(2)}, u32[]{:S(2)}) async-start(bf16[16,12,256]{2,1,0:T(8,128)(2,1)} %reshape.67), calls=%async_computation.1 | async-start | bytes 262144 | tf_op jit(solution)/shard_map/all_to_all | solution.py:8
  347.0 42.3 %all-gather.3.cloned.1.call-done = bf16[32,6,3584]{2,1,0:T(8,128)(2,1)} async-done(((bf16[1,6,3584]{2,1,0:T(8,128)(2,1)}), bf16[32,6,3584]{2,1,0:T(8,128)(2,1)}) %all-gather.3.cloned.1.call-update) | async-done | bytes 1376272 | tf_op jit(solution)/shard_map/all_gather | solution.py:84
  389.3 2.4 reshape.94
  393.2 8.9 %all-to-all-start.3 = ((bf16[16,12,256]{2,1,0:T(8,128)(2,1)}), bf16[16,12,256]{2,1,0:T(8,128)(2,1)S(1)}, u32[]{:S(2)}, u32[]{:S(2)}) async-start(bf16[16,12,256]{2,1,0:T(8,128)(2,1)} %reshape.71), calls=%async_computation.3 | async-start | bytes 262144 | tf_op jit(solution)/shard_map/all_to_all | solution.py:8
  403.0 7.2 %all-to-all-done.3 = bf16[16,12,256]{2,1,0:T(8,128)(2,1)S(1)} async-done(((bf16[16,12,256]{2,1,0:T(8,128)(2,1)}), bf16[16,12,256]{2,1,0:T(8,128)(2,1)S(1)}, u32[]{:S(2)}, u32[]{:S(2)}) %all-to-all-start.3) | async-done | bytes 98336 | tf_op jit(solution)/shard_map/all_to_all | solution.py:8
  (54 shorter events, 10.3 us)
Async XLA Ops:
  7.2 22.5 %copy-start = (bf16[1,256,3584]{2,1,0:T(8,128)(2,1)S(1)}, bf16[1,256,3584]{2,1,0:T(8,128)(2,1)}, u32[]{:S(2)}) copy-start(bf16[1,256,3584]{2,1,0:T(8,128)(2,1)} %param.9) | copy-start | bytes 5505028
  7.2 325.9 %all-reduce.4.cloned.1.call-start = ((), (), s32[]{:S(2)}) async-start(), calls=%async_computation.4 | async-start | bytes 5505024 | tf_op jit(solution)/shard_map/psum | solution.py:57
  31.8 0.8 copy-start.1
  31.8 0.9 copy-start.2
  31.8 357.5 %all-gather.3.cloned.1.call-start = ((), (), s32[]{:S(2)}) async-start(), calls=%async_computation.5 | async-start | bytes 1892352 | tf_op jit(solution)/shard_map/all_gather | solution.py:84
  135.4 13.4 %collective-permute-start.6 = (f32[8,1792]{1,0:T(8,128)S(1)}, f32[8,1792]{1,0:T(8,128)S(1)}, u32[]{:S(2)}, u32[]{:S(2)}) collective-permute-start(f32[8,1792]{1,0:T(8,128)S(1)} %fusion), channel_id=1, source_target_pairs={{0,112},{16,128},{32,144},{48,160},{64,176},{80,192},{96,208},{112... | collective-permute-start | bytes 172040
  136.7 19.1 %collective-permute-start.5 = (f32[8,1792]{1,0:T(8,128)S(1)}, f32[8,1792]{1,0:T(8,128)S(1)}, u32[]{:S(2)}, u32[]{:S(2)}) collective-permute-start(f32[8,1792]{1,0:T(8,128)S(1)} %fusion), channel_id=1, source_target_pairs={{0,96},{16,112},{32,128},{48,144},{64,160},{80,176},{96,192},{112,... | collective-permute-start | bytes 172040
  138.0 9.5 %collective-permute-start.7 = (f32[6,1792]{1,0:T(8,128)S(1)}, f32[6,1792]{1,0:T(8,128)S(1)}, u32[]{:S(2)}, u32[]{:S(2)}) collective-permute-start(f32[6,1792]{1,0:T(8,128)S(1)} %slice.22), channel_id=1, source_target_pairs={{0,128},{16,144},{32,160},{48,176},{64,192},{80,208},{96,224},{112... | collective-permute-start | bytes 129032
  139.3 22.2 %collective-permute-start.4 = (f32[8,1792]{1,0:T(8,128)S(1)}, f32[8,1792]{1,0:T(8,128)S(1)}, u32[]{:S(2)}, u32[]{:S(2)}) collective-permute-start(f32[8,1792]{1,0:T(8,128)S(1)} %fusion), channel_id=1, source_target_pairs={{0,80},{16,96},{32,112},{48,128},{64,144},{80,160},{96,176},{112,1... | collective-permute-start | bytes 172040
  140.6 20.9 %collective-permute-start.3 = (f32[8,1792]{1,0:T(8,128)S(1)}, f32[8,1792]{1,0:T(8,128)S(1)}, u32[]{:S(2)}, u32[]{:S(2)}) collective-permute-start(f32[8,1792]{1,0:T(8,128)S(1)} %fusion), channel_id=1, source_target_pairs={{0,64},{16,80},{32,96},{48,112},{64,128},{80,144},{96,160},{112,17... | collective-permute-start | bytes 172040
  147.5 14.1 %collective-permute-start.2 = (f32[8,1792]{1,0:T(8,128)S(1)}, f32[8,1792]{1,0:T(8,128)S(1)}, u32[]{:S(2)}, u32[]{:S(2)}) collective-permute-start(f32[8,1792]{1,0:T(8,128)S(1)} %fusion), channel_id=1, source_target_pairs={{0,48},{16,64},{32,80},{48,96},{64,112},{80,128},{96,144},{112,160... | collective-permute-start | bytes 172040
  148.8 12.8 %collective-permute-start.1 = (f32[8,1792]{1,0:T(8,128)S(1)}, f32[8,1792]{1,0:T(8,128)S(1)}, u32[]{:S(2)}, u32[]{:S(2)}) collective-permute-start(f32[8,1792]{1,0:T(8,128)S(1)} %fusion), channel_id=1, source_target_pairs={{0,32},{16,48},{32,64},{48,80},{64,96},{80,112},{96,128},{112,144}... | collective-permute-start | bytes 172040
  155.8 5.8 %collective-permute-start = (f32[8,1792]{1,0:T(8,128)S(1)}, f32[8,1792]{1,0:T(8,128)S(1)}, u32[]{:S(2)}, u32[]{:S(2)}) collective-permute-start(f32[8,1792]{1,0:T(8,128)S(1)} %fusion), channel_id=1, source_target_pairs={{0,16},{16,32},{32,48},{48,64},{64,80},{80,96},{96,112},{112,128},... | collective-permute-start | bytes 172040
  338.0 55.2 %all-to-all-start.1 = ((bf16[16,12,256]{2,1,0:T(8,128)(2,1)}), bf16[16,12,256]{2,1,0:T(8,128)(2,1)S(1)}, u32[]{:S(2)}, u32[]{:S(2)}) async-start(bf16[16,12,256]{2,1,0:T(8,128)(2,1)} %reshape.67), calls=%async_computation.1 | async-start | bytes 262144 | tf_op jit(solution)/shard_map/all_to_all | solution.py:8
  393.2 16.9 %all-to-all-start.3 = ((bf16[16,12,256]{2,1,0:T(8,128)(2,1)}), bf16[16,12,256]{2,1,0:T(8,128)(2,1)S(1)}, u32[]{:S(2)}, u32[]{:S(2)}) async-start(bf16[16,12,256]{2,1,0:T(8,128)(2,1)} %reshape.71), calls=%async_computation.3 | async-start | bytes 262144 | tf_op jit(solution)/shard_map/all_to_all | solution.py:8
Sparse Core Ops, SparseCore 0:
  31.9 301.1 all-reduce.3
  336.2 53.0 all-gather.2
where the time goes:
time: 421 us; the launch traced here: 420 us
  waiting for transfers between devices  220 us (52%)
  blocking collectives  119 us (28%)
  starting transfers between devices  42 us (10%)
  between operations  15 us (4%)
  local copies, waits for them, and re-layouts  10.3 us (2%)
  matrix products  8.25 us (2%)
  other arithmetic  4.63 us (1%)
    psum x1, waiting for transfers between devices, local(): lax.psum(jnp.dot(token_slots, w_gate_up, preferred_element_type=jnp.float...  171 us
    unnamed x1, blocking collectives  88.8 us
    all_gather x1, waiting for transfers between devices, local(): lax.all_gather(pre_grad, 'dp', axis=0, tiled=True)  42.3 us
    all_to_all x2, blocking collectives, swap_blocks(): lax.all_to_all(blocks, 'expert', split_axis=0, concat_axis=0, tiled=True)  30.5 us
    unnamed x8, starting transfers between devices  24.1 us
    all_to_all x2, starting transfers between devices, swap_blocks(): lax.all_to_all(blocks, 'expert', split_axis=0, concat_axis=0, tiled=True)  17.8 us
  transfers between devices with their start and end apart: 12, of which 3 were waited for; matrix products, arithmetic and copies ran while one was open for 24% of the time, Pallas kernels for 0%

commit v1 on v0

v1 whole, which is shorter than its diff:
```python
import functools

import jax
import jax.numpy as jnp
from jax import lax
from jax.experimental import pallas as pl
from jax.experimental.pallas import tpu as pltpu
from jax.sharding import Mesh, PartitionSpec as P

BF16 = jnp.bfloat16
F32 = jnp.float32
NX, NY, NC, NL, NZ = 4, 4, 2, 2, 8
TOK, TOPK, E, CAP = 64, 2, 16, 12
PAIR = 2 * CAP
ROWS = E * CAP
SEND = E * PAIR
DW = 256
F = 1792
H = F // NC
RX = ROWS // NX
VMEM = pl.BlockSpec(memory_space=pltpu.VMEM)


def mm(a, b):
    return lax.dot_general(a, b, (((1,), (0,)), ((), ())), preferred_element_type=F32)


def mm_t(a, b):
    return lax.dot_general(a, b, (((1,), (1,)), ((), ())), preferred_element_type=F32)


def iota(shape, dim):
    return lax.broadcasted_iota(jnp.int32, shape, dim)


def onehot(cond):
    return jnp.where(cond, 1.0, 0.0).astype(BF16)


def call(kernel, out_shape, count, limit_mb=12):
    return pl.pallas_call(
        kernel,
        out_shape=out_shape,
        in_specs=[VMEM] * count,
        out_specs=jax.tree.map(lambda _: VMEM, out_shape),
        compiler_params=pltpu.CompilerParams(vmem_limit_bytes=limit_mb << 20),
    )


def pack_kernel(ids_ref, gate_ref, tok_ref, grad_ref, send_ref, place_ref):
    ids = ids_ref[...]
    hots = [(ids[:, k : k + 1] == iota((TOK, E), 1)).astype(F32) for k in range(TOPK)]
    lower = onehot(iota((TOK, TOK), 1) < iota((TOK, TOK), 0))
    earlier = mm(lower, (hots[0] + hots[1]).astype(BF16))
    eye = iota((TOK, TOK), 0) == iota((TOK, TOK), 1)
    row = iota((SEND, TOK), 0)
    grad = grad_ref[...].astype(F32)
    pick_tok = jnp.zeros((SEND, TOK), BF16)
    total = jnp.zeros((SEND, DW), F32)
    places = []
    for k in range(TOPK):
        rank = jnp.sum(hots[k] * earlier, axis=1, keepdims=True).astype(jnp.int32)
        place = ids[:, k : k + 1] * PAIR + rank
        places.append(place)
        across = jnp.sum(jnp.where(eye, place, 0), axis=0, keepdims=True)
        pick_tok += onehot(row == across)
        scaled = (gate_ref[:, k : k + 1] * grad).astype(BF16)
        total += mm(onehot(row == across + CAP), scaled)
    total += mm(pick_tok, tok_ref[...])
    send_ref[...] = total.astype(BF16)
    place_ref[...] = jnp.concatenate(places, axis=1)


def slot_to_pair(slot):
    extra = jnp.zeros_like(slot)
    for b in range(1, E):
        extra += jnp.where(slot >= b * CAP, CAP, 0)
    return slot + extra


def half_columns(c):
    return pl.ds(pl.multiple_of(c * H, H), H), pl.ds(pl.multiple_of(F + c * H, H), H)


def partials(x, g, wgu_ref, wd_ref, c):
    gate, up = half_columns(c)
    return mm(x, wgu_ref[:, gate]), mm(x, wgu_ref[:, up]), mm_t(g, wd_ref[gate, :])


def away_kernel(arr_ref, wgu_ref, wd_ref, out_ref, x_ref, g_ref):
    arrived = arr_ref[...]
    source = slot_to_pair(iota((ROWS, 1), 0))
    col = iota((ROWS, SEND), 1)
    x_ref[...] = mm(onehot(col == source), arrived).astype(BF16)
    g_ref[...] = mm(onehot(col == source + CAP), arrived).astype(BF16)
    terms = partials(x_ref[...], g_ref[...], wgu_ref, wd_ref, 1 - lax.axis_index("c"))
    for j, term in enumerate(terms):
        out_ref[:, j * H : (j + 1) * H] = term.astype(BF16)


def home_kernel(x_ref, g_ref, wgu_ref, wd_ref, got_ref, out_ref, own_ref):
    c, i = lax.axis_index("c"), lax.axis_index("x")
    terms = partials(x_ref[...], g_ref[...], wgu_ref, wd_ref, c)
    for j, term in enumerate(terms):
        cols = slice(j * H, (j + 1) * H)
        out_ref[:, cols] = (term + got_ref[:, cols].astype(F32)).astype(BF16)
    rows = pl.ds(pl.multiple_of(i * RX, RX), RX)
    terms = partials(x_ref[rows, :], g_ref[rows, :], wgu_ref, wd_ref, c)
    for j, term in enumerate(terms):
        cols = slice(j * H, (j + 1) * H)
        own_ref[:, cols] = term + got_ref[rows, cols].astype(F32)


def sum_x_kernel(got_ref, own_ref, out_ref, rest_ref):
    i = lax.axis_index("x")
    total = own_ref[...] - got_ref[i].astype(F32)
    for j in range(NX):
        total += got_ref[j].astype(F32)
    rounded = total.astype(BF16)
    out_ref[...] = rounded
    rest_ref[...] = total - rounded.astype(F32)


def act_kernel(part_ref, rest_ref, out_ref):
    total = rest_ref[...]
    for i in range(NY):
        total += part_ref[i].astype(F32)
    gate, up, hg = total[:, :H], total[:, H : 2 * H], total[:, 2 * H :]
    sig = jax.nn.sigmoid(gate)
    silu = gate * sig
    out_ref[:, :H] = (silu * up).astype(BF16)
    out_ref[:, H : 2 * H] = (hg * up * sig * (1.0 + gate * (1.0 - sig))).astype(BF16)
    out_ref[:, 2 * H :] = (hg * silu).astype(BF16)


def finish_kernel(act_ref, wgu_ref, wd_ref, send_ref):
    act = act_ref[...].reshape(NX, NC, RX, 3 * H)
    out = jnp.zeros((ROWS, DW), F32)
    back = jnp.zeros((ROWS, DW), F32)
    for c in range(NC):
        a = act[:, c].reshape(ROWS, 3 * H)
        out += mm(a[:, :H], wd_ref[c * H : (c + 1) * H, :])
        back += mm_t(a[:, H : 2 * H], wgu_ref[:, c * H : (c + 1) * H])
        back += mm_t(a[:, 2 * H :], wgu_ref[:, F + c * H : F + (c + 1) * H])
    row = iota((SEND, ROWS), 0)
    target = jnp.where(iota((1, ROWS), 1) >= 0, slot_to_pair(iota((1, ROWS), 1)), 0)
    send = mm(onehot(row == target), out.astype(BF16))
    send += mm(onehot(row == target + CAP), back.astype(BF16))
    send_ref[...] = send.astype(BF16)


def combine_kernel(ret_ref, gate_ref, place_ref, moe_ref, tok_ref):
    returned = ret_ref[...]
    col = iota((TOK, SEND), 1)
    place = place_ref[...]
    moe = jnp.zeros((TOK, DW), F32)
    pick = jnp.zeros((TOK, SEND), BF16)
    for k in range(TOPK):
        at = place[:, k : k + 1]
        moe += gate_ref[:, k : k + 1] * mm(onehot(col == at), returned)
        pick += onehot(col == at + CAP)
    moe_ref[...] = moe.astype(BF16)
    tok_ref[...] = mm(pick, returned).astype(BF16)


def local(tokens, gate_up, down, expert_ids, gate_values, out_grad):
    wgu, wd = gate_up[0], down[0]
    send, place = call(
        pack_kernel,
        (jax.ShapeDtypeStruct((SEND, DW), BF16), jax.ShapeDtypeStruct((TOK, TOPK), jnp.int32)),
        4,
    )(expert_ids, gate_values, tokens, out_grad)
    arrived = lax.all_to_all(
        send.reshape(E, PAIR, DW), ("yl", "z"), 0, 0, tiled=True
    ).reshape(SEND, DW)
    wide, narrow = jax.ShapeDtypeStruct((ROWS, 3 * H), BF16), jax.ShapeDtypeStruct((ROWS, DW), BF16)
    chunk16, chunk32 = (jax.ShapeDtypeStruct((RX, 3 * H), t) for t in (BF16, F32))
    away, x, g = call(away_kernel, (wide, narrow, narrow), 3)(arrived, wgu, wd)
    got = lax.ppermute(away, "c", [(0, 1), (1, 0)])
    chip, own = call(home_kernel, (wide, chunk32), 5)(x, g, wgu, wd, got)
    got = lax.all_to_all(chip.reshape(NX, RX, 3 * H), "x", 0, 0, tiled=True)
    chunk, rest = call(sum_x_kernel, (chunk16, chunk32), 2)(got, own)
    parts = lax.all_gather(chunk, "yh", axis=0)
    act = call(act_kernel, chunk16, 2)(parts, rest)
    acts = lax.all_gather(act, ("x", "c"), axis=0)
    back = call(finish_kernel, jax.ShapeDtypeStruct((SEND, DW), BF16), 3)(acts, wgu, wd)
    returned = lax.all_to_all(
        back.reshape(E, PAIR, DW), ("yl", "z"), 0, 0, tiled=True
    ).reshape(SEND, DW)
    shape = jax.ShapeDtypeStruct((TOK, DW), BF16)
    return call(combine_kernel, (shape, shape), 3)(returned, gate_values, place)


def solution(mesh):
    fine = Mesh(mesh.devices.reshape(NX, NY, NC, NL, NZ), ("x", "yh", "c", "yl", "z"))
    dp, ex = ("x", "yh", "c"), ("yl", "z")
    return jax.shard_map(
        local,
        mesh=fine,
        in_specs=(
            P(ex, dp),
            P(ex, dp, None),
            P(ex, None, dp),
            P(ex, None),
            P(ex, None),
            P(ex, dp),
        ),
        out_specs=(P(ex, dp), P(ex, dp)),
        check_vma=False,
    )
```

time: 421 us -> 137 us (0.33)
  waiting for transfers between devices: 220 us -> 27.6 us
  starting transfers between devices: 42 us -> 2.09 us
  blocking collectives: 119 us -> 79.5 us
  matrix products: 8.25 us -> 0 us
  Pallas kernels: 0 us -> 5.58 us
  other arithmetic: 4.63 us -> 0 us
    psum x1 -> x0, waiting for transfers between devices: 171 us -> none  [local(): lax.psum(jnp.dot(token_slots, w_gate_up, preferred_element_type=jnp.float...]
    unnamed x1 -> x0, blocking collectives: 88.8 us -> none
    all_to_all x2 -> x3, blocking collectives: 30.5 us -> 56.9 us  [the longest x1 20.1 us: local(): lax.all_to_all(send.reshape(E, PAIR, DW), ('yl', 'z'), 0, 0, tiled=True)]
    unnamed x8 -> x0, starting transfers between devices: 24.1 us -> none
    all_gather x0 -> x1, blocking collectives: none -> 22.6 us  [local(): parts = lax.all_gather(chunk, 'yh', axis=0)]
    all_to_all x2 -> x0, starting transfers between devices: 17.8 us -> none  [swap_blocks(): lax.all_to_all(blocks, 'expert', split_axis=0, concat_axis=0, tiled=True)]
    all_gather x1, waiting for transfers between devices: 42.3 us -> 24.9 us  [local(): acts = lax.all_gather(act, ('x', 'c'), axis=0)]
    dot_general x6 -> x0, matrix products: 8.25 us -> none  [the longest x1 2.51 us: local(): jnp.dot(hidden, w_down, preferred_element_type=jnp.float32)]
  transfers between devices with their start and end apart: 12 -> 2, of which waited for: 3 -> 2; matrix products, arithmetic and copies ran while one was open for 24% -> 0% of each run, Pallas kernels for 0% -> 0%
where the time goes in v1:
time: 137 us; the launch traced here: 136 us
  blocking collectives  79.5 us (58%)
  waiting for transfers between devices  27.6 us (20%)
  between operations  14.1 us (10%)
  local copies, waits for them, and re-layouts  7.32 us (5%)
  Pallas kernels  5.58 us (4%)
  starting transfers between devices  2.09 us (2%)
    all_gather x1, waiting for transfers between devices, local(): acts = lax.all_gather(act, ('x', 'c'), axis=0)  24.9 us
    all_gather x1, blocking collectives, local(): parts = lax.all_gather(chunk, 'yh', axis=0)  22.6 us
    all_to_all x1, blocking collectives, local(): lax.all_to_all(send.reshape(E, PAIR, DW), ('yl', 'z'), 0, 0, tiled=True)  20.1 us
    all_to_all x1, blocking collectives, local(): got = lax.all_to_all(chip.reshape(NX, RX, 3 * H), 'x', 0, 0, tiled=True)  19.3 us
    all_to_all x1, blocking collectives, local(): lax.all_to_all(back.reshape(E, PAIR, DW), ('yl', 'z'), 0, 0, tiled=True)  17.5 us
    unnamed x16, local copies, waits for them, and re-layouts  7.32 us
  transfers between devices with their start and end apart: 2, of which 2 were waited for; matrix products, arithmetic and copies ran while one was open for 0% of the time, Pallas kernels for 0%

profile of v1, /device:TPU:8, one launch (start us, length us, event | category | flops | bytes accessed | tf_op | source)
XLA Modules:
  0.0 136.1 jit_solution(7743281909179195514)
XLA Ops:
  7.2 0.0 all-gather.4.cloned.1.call-start
  7.2 0.8 copy.9.gate_ref
  8.0 0.8 copy.8.ids_ref
  8.7 0.8 copy-done.5
  9.5 0.8 copy-done.6
  10.3 0.7 shard_map.77
  11.0 20.1 %all_to_all.15 = bf16[16,24,256]{2,1,0:T(8,128)(2,1)S(1)} all-to-all(bf16[16,24,256]{2,1,0:T(8,128)(2,1)S(1)} %bitcast.21), channel_id=1, replica_groups=mesh['x'=4,'yh'=4,'c'=2,'yl'=2,'z'=8] {'yl','z'}, dimensions={0} | all-to-all | bytes 393216 | tf_op jit(solution)/shard_map/all_to_all | solution.py:173
  31.1 1.5 %copy-done = bf16[1,256,3584]{2,1,0:T(8,128)(2,1)S(1)} copy-done((bf16[1,256,3584]{2,1,0:T(8,128)(2,1)S(1)}, bf16[1,256,3584]{2,1,0:T(8,128)(2,1)}, u32[]{:S(2)}) %copy-start) | copy-done | bytes 1835032
  32.6 1.2 copy-done.2
  33.7 0.7 shard_map.78
  34.5 2.1 %collective-permute-start = (bf16[192,2688]{1,0:T(8,128)(2,1)S(1)}, bf16[192,2688]{1,0:T(8,128)(2,1)S(1)}, u32[]{:S(2)}, u32[]{:S(2)}) collective-permute-start(bf16[192,2688]{1,0:T(8,128)(2,1)S(1)} %get-tuple-element.14), channel_id=1, source_target_pairs={{0,16},{16,0},{1,17},{17,1},{2,18},{18,2},{3,19},{19,3},{4,20},{20... | collective-permute-start | bytes 3096584 | tf_op jit(solution)/shard_map/ppermute | solution.py:179
  36.5 2.6 %collective-permute-done.got_ref = bf16[192,2688]{1,0:T(8,128)(2,1)S(1)} collective-permute-done((bf16[192,2688]{1,0:T(8,128)(2,1)S(1)}, bf16[192,2688]{1,0:T(8,128)(2,1)S(1)}, u32[]{:S(2)}, u32[]{:S(2)}) %collective-permute-start) | collective-permute-done | bytes 1032224 | tf_op jit(solution)/shard_map/ppermute | solution.py:179
  39.1 0.0 copy-done.1
  39.1 0.8 shard_map.79
  39.9 19.3 %all_to_all.16.got_ref = bf16[4,48,2688]{2,1,0:T(8,128)(2,1)S(1)} all-to-all(bf16[4,48,2688]{2,1,0:T(8,128)(2,1)S(1)} %bitcast.17), channel_id=1, replica_groups=mesh['x'=4,'yh'=4,'c'=2,'yl'=2,'z'=8] {'x'}, dimensions={0} | all-to-all | bytes 2064384 | tf_op jit(solution)/shard_map/all_to_all | solution.py:181
  59.2 0.3 shard_map.80
  59.5 22.6 %all-gather = bf16[192,2688]{1,0:T(8,128)(2,1)S(1)} all-gather(bf16[48,2688]{1,0:T(8,128)(2,1)S(1)} %get-tuple-element.17), channel_id=2, replica_groups=mesh['x'=4,'yh'=4,'c'=2,'yl'=2,'z'=8] {'yh'}, dimensions={0}, use_global_device_ids=true | all-gather | bytes 1290240 | tf_op jit(solution)/shard_map/all_gather | solution.py:183
  82.0 0.9 shard_map.81
  83.0 0.0 all-gather.4.cloned.1.call-update
  83.0 24.9 %all-gather.4.cloned.1.call-done = bf16[384,2688]{1,0:T(8,128)(2,1)} async-done(((bf16[48,2688]{1,0:T(8,128)(2,1)}), bf16[384,2688]{1,0:T(8,128)(2,1)}) %all-gather.4.cloned.1.call-update) | async-done | bytes 2064400 | tf_op jit(solution)/shard_map/all_gather | solution.py:185
  107.9 1.6 %copy-done.4 = bf16[384,2688]{1,0:T(8,128)(2,1)S(1)} copy-done((bf16[384,2688]{1,0:T(8,128)(2,1)S(1)}, bf16[384,2688]{1,0:T(8,128)(2,1)}, u32[]{:S(2)}) %copy-start.4) | copy-done | bytes 2064408
  109.5 1.3 shard_map.82
  110.8 17.5 %all_to_all.17 = bf16[16,24,256]{2,1,0:T(8,128)(2,1)S(1)} all-to-all(bf16[16,24,256]{2,1,0:T(8,128)(2,1)S(1)} %bitcast.18), channel_id=1, replica_groups=mesh['x'=4,'yh'=4,'c'=2,'yl'=2,'z'=8] {'yl','z'}, dimensions={0} | all-to-all | bytes 393216 | tf_op jit(solution)/shard_map/all_to_all | solution.py:187
  128.4 0.9 shard_map.83
  (8 shorter events, 0.0 us)
Async XLA Ops:
  7.2 100.8 %all-gather.4.cloned.1.call-start = ((), (), s32[]{:S(2)}) async-start(), calls=%async_computation.3 | async-start | bytes 2322432 | tf_op jit(solution)/shard_map/all_gather | solution.py:185
  8.7 0.8 copy-start.5
  9.5 0.8 copy-start.6
  31.1 1.5 %copy-start = (bf16[1,256,3584]{2,1,0:T(8,128)(2,1)S(1)}, bf16[1,256,3584]{2,1,0:T(8,128)(2,1)}, u32[]{:S(2)}) copy-start(bf16[1,256,3584]{2,1,0:T(8,128)(2,1)} %param.7) | copy-start | bytes 5505028
  32.6 1.2 copy-start.2
  33.7 5.4 %copy-start.1 = (bf16[1,256,3584]{2,1,0:T(8,128)(2,1)S(1)}, bf16[1,256,3584]{2,1,0:T(8,128)(2,1)}, u32[]{:S(2)}) copy-start(bf16[1,256,3584]{2,1,0:T(8,128)(2,1)} %param.7) | copy-start | bytes 5505028
  33.7 5.4 %copy-start.3 = (bf16[1,1792,256]{2,1,0:T(8,128)(2,1)S(1)}, bf16[1,1792,256]{2,1,0:T(8,128)(2,1)}, u32[]{:S(2)}) copy-start(bf16[1,1792,256]{2,1,0:T(8,128)(2,1)} %param.8) | copy-start | bytes 2752516
  34.5 4.7 %collective-permute-start = (bf16[192,2688]{1,0:T(8,128)(2,1)S(1)}, bf16[192,2688]{1,0:T(8,128)(2,1)S(1)}, u32[]{:S(2)}, u32[]{:S(2)}) collective-permute-start(bf16[192,2688]{1,0:T(8,128)(2,1)S(1)} %get-tuple-element.14), channel_id=1, source_target_pairs={{0,16},{16,0},{1,17},{17,1},{2,18},{18,2},{3,19},{19,3},{4,20},{20... | collective-permute-start | bytes 3096584 | tf_op jit(solution)/shard_map/ppermute | solution.py:179
  107.9 1.6 %copy-start.4 = (bf16[384,2688]{1,0:T(8,128)(2,1)S(1)}, bf16[384,2688]{1,0:T(8,128)(2,1)}, u32[]{:S(2)}) copy-start(bf16[384,2688]{1,0:T(8,128)(2,1)} %all-gather.4.cloned.1.call-done) | copy-start | bytes 6193156
Sparse Core Ops, SparseCore 0:
  83.1 24.7 all-gather.3

commit v2 on v1

v2 whole, which is shorter than its diff:
```python
import jax
import jax.numpy as jnp
from jax import lax
from jax.experimental import pallas as pl
from jax.experimental.pallas import tpu as pltpu
from jax.sharding import PartitionSpec as P

BF16 = jnp.bfloat16
F32 = jnp.float32
NX, NY, NC = 4, 4, 2
RING = 4

TOK, TOPK, E, CAP = 64, 2, 16, 12
PAIR = 2 * CAP
ROWS = E * CAP
SEND = E * PAIR
DW = 256
F = 1792
H = F // NC
RX = ROWS // RING

ALONG_X = [[[(x * NY + y) * NC + c for x in range(NX)] for y in range(NY)] for c in range(NC)]
ALONG_Y = [[[(x * NY + y) * NC + c for y in range(NY)] for x in range(NX)] for c in range(NC)]
FIRST = ALONG_X[0] + ALONG_Y[1]
SECOND = ALONG_Y[0] + ALONG_X[1]
SWAP = [(i, i ^ 1) for i in range(NX * NY * NC)]
VMEM = pl.BlockSpec(memory_space=pltpu.VMEM)


def core():
    return lax.rem(lax.axis_index("dp"), NC)


def place_in_first():
    d = lax.axis_index("dp")
    x, y = lax.div(d, NY * NC), lax.rem(lax.div(d, NC), NY)
    return jnp.where(core() == 0, x, y)


def mm(a, b):
    return lax.dot_general(a, b, (((1,), (0,)), ((), ())), preferred_element_type=F32)


def mm_t(a, b):
    return lax.dot_general(a, b, (((1,), (1,)), ((), ())), preferred_element_type=F32)


def iota(shape, dim):
    return lax.broadcasted_iota(jnp.int32, shape, dim)


def onehot(cond):
    return jnp.where(cond, 1.0, 0.0).astype(BF16)


def call(kernel, out_shape, count, limit_mb=12, flops=0, nbytes=0, **kw):
    kw.setdefault("in_specs", [VMEM] * count)
    return pl.pallas_call(
        kernel,
        out_shape=out_shape,
        out_specs=jax.tree.map(lambda _: VMEM, out_shape),
        compiler_params=pltpu.CompilerParams(vmem_limit_bytes=limit_mb << 20),
        cost_estimate=pl.CostEstimate(flops=flops, bytes_accessed=nbytes, transcendentals=0),
        **kw,
    )


def turned(row, eye):
    return jnp.sum(jnp.where(eye, row, jnp.zeros_like(row)), axis=1, keepdims=True)


def pack_kernel(
    ids_hbm, gate_hbm, tok_hbm, grad_hbm, wgu_hbm, wd_hbm,
    send_ref, place_ref, weight_ref, wgu_out, wd_out,
    ids_ref, gate_ref, tok_ref, grad_ref, sems,
):
    pairs = [(ids_hbm, ids_ref), (gate_hbm, gate_ref), (tok_hbm, tok_ref), (grad_hbm, grad_ref)]
    pairs += [(wgu_hbm, wgu_out), (wd_hbm, wd_out)]
    moves = [pltpu.make_async_copy(*pair, sems.at[n]) for n, pair in enumerate(pairs)]
    for move in moves:
        move.start()
    eye = iota((TOK, TOK), 0) == iota((TOK, TOK), 1)
    before = onehot(iota((TOK, TOK), 0) < iota((TOK, TOK), 1))
    row = iota((SEND, TOK), 0)
    moves[0].wait()
    moves[1].wait()
    ids = ids_ref[...]
    hots = [(ids[k : k + 1, :] == iota((E, TOK), 0)).astype(F32) for k in range(TOPK)]
    earlier = mm((hots[0] + hots[1]).astype(BF16), before)
    across, places, weights = [], [], []
    for k in range(TOPK):
        rank = jnp.sum(hots[k] * earlier, axis=0, keepdims=True).astype(jnp.int32)
        place = ids[k : k + 1, :] * PAIR + rank
        across.append(place)
        places.append(turned(place, eye))
        weights.append(turned(gate_ref[k : k + 1, :], eye))
    place_ref[...] = jnp.concatenate(places, axis=1)
    weight_ref[...] = jnp.concatenate(weights, axis=1)
    moves[2].wait()
    pick_tok = onehot((row == across[0]) | (row == across[1]))
    total = mm(pick_tok, tok_ref[...])
    moves[3].wait()
    grad = grad_ref[...].astype(F32)
    for k in range(TOPK):
        total += mm(onehot(row == across[k] + CAP), (weights[k] * grad).astype(BF16))
    send_ref[...] = total.astype(BF16)
    for move in moves[4:]:
        move.wait()


def slot_to_pair(slot):
    extra = jnp.zeros_like(slot)
    for b in range(1, E):
        extra += jnp.where(slot >= b * CAP, CAP, 0)
    return slot + extra


def half_columns(c):
    return pl.ds(pl.multiple_of(c * H, H), H), pl.ds(pl.multiple_of(F + c * H, H), H)


def partials(x, g, wgu_ref, wd_ref, c):
    gate, up = half_columns(c)
    return mm(x, wgu_ref[:, gate]), mm(x, wgu_ref[:, up]), mm_t(g, wd_ref[gate, :])


def away_kernel(arr_ref, wgu_ref, wd_ref, out_ref, x_ref, g_ref):
    arrived = arr_ref[...]
    source = slot_to_pair(iota((ROWS, 1), 0))
    col = iota((ROWS, SEND), 1)
    x_ref[...] = mm(onehot(col == source), arrived).astype(BF16)
    g_ref[...] = mm(onehot(col == source + CAP), arrived).astype(BF16)
    terms = partials(x_ref[...], g_ref[...], wgu_ref, wd_ref, 1 - core())
    for j, term in enumerate(terms):
        out_ref[:, j * H : (j + 1) * H] = term.astype(BF16)


def home_kernel(x_ref, g_ref, wgu_ref, wd_ref, out_ref):
    terms = partials(x_ref[...], g_ref[...], wgu_ref, wd_ref, core())
    for j, term in enumerate(terms):
        out_ref[:, j * H : (j + 1) * H] = term


def add_kernel(home_ref, got_ref, out_ref, own_ref):
    out_ref[...] = (home_ref[...] + got_ref[...].astype(F32)).astype(BF16)
    rows = pl.ds(pl.multiple_of(place_in_first() * RX, RX), RX)
    own_ref[...] = home_ref[rows, :] + got_ref[rows, :].astype(F32)


def sum_kernel(got_ref, own_ref, out_ref, rest_ref):
    i = place_in_first()
    total = own_ref[...] - got_ref[i].astype(F32)
    for j in range(RING):
        total += got_ref[j].astype(F32)
    rounded = total.astype(BF16)
    out_ref[...] = rounded
    rest_ref[...] = total - rounded.astype(F32)


def act_kernel(part_ref, rest_ref, out_ref):
    total = rest_ref[...]
    for i in range(RING):
        total += part_ref[i].astype(F32)
    gate, up, hg = total[:, :H], total[:, H : 2 * H], total[:, 2 * H :]
    sig = jax.nn.sigmoid(gate)
    silu = gate * sig
    out_ref[:, :H] = (silu * up).astype(BF16)
    out_ref[:, H : 2 * H] = (hg * up * sig * (1.0 + gate * (1.0 - sig))).astype(BF16)
    out_ref[:, 2 * H :] = (hg * silu).astype(BF16)


def products(act_ref, wgu_ref, wd_ref, c):
    gate, up = half_columns(c)
    out = mm(act_ref[:, :H], wd_ref[gate, :])
    back = mm_t(act_ref[:, H : 2 * H], wgu_ref[:, gate])
    return out, back + mm_t(act_ref[:, 2 * H :], wgu_ref[:, up])


def first_kernel(act_ref, wgu_ref, wd_ref, out_ref, back_ref):
    out_ref[...], back_ref[...] = products(act_ref, wgu_ref, wd_ref, core())


def finish_kernel(act_ref, wgu_ref, wd_ref, out_ref, back_ref, send_ref):
    out, back = products(act_ref, wgu_ref, wd_ref, 1 - core())
    row = iota((SEND, ROWS), 0)
    target = slot_to_pair(iota((1, ROWS), 1))
    send = mm(onehot(row == target), (out_ref[...] + out).astype(BF16))
    send += mm(onehot(row == target + CAP), (back_ref[...] + back).astype(BF16))
    send_ref[...] = send.astype(BF16)


def combine_kernel(ret_ref, weight_ref, place_ref, moe_ref, tok_ref):
    returned = ret_ref[...]
    col = iota((TOK, SEND), 1)
    place = place_ref[...]
    moe = jnp.zeros((TOK, DW), F32)
    pick = jnp.zeros((TOK, SEND), BF16)
    for k in range(TOPK):
        at = place[:, k : k + 1]
        moe += weight_ref[:, k : k + 1] * mm(onehot(col == at), returned)
        pick += onehot(col == at + CAP)
    moe_ref[...] = moe.astype(BF16)
    tok_ref[...] = mm(pick, returned).astype(BF16)


def local(tokens, gate_up, down, expert_ids, gate_values, out_grad):
    sds = jax.ShapeDtypeStruct
    wide16, wide32 = (sds((ROWS, 3 * H), t) for t in (BF16, F32))
    narrow16, narrow32 = (sds((ROWS, DW), t) for t in (BF16, F32))
    chunk16, chunk32 = (sds((RX, 3 * H), t) for t in (BF16, F32))
    small = [pltpu.VMEM((TOPK, TOK), jnp.int32), pltpu.VMEM((TOPK, TOK), F32)]
    small += [pltpu.VMEM((TOK, DW), BF16)] * 2
    work = dict(flops=2 * ROWS * DW * 3 * H, nbytes=4 << 20)

    send, place, weight, wgu, wd = call(
        pack_kernel,
        (
            sds((SEND, DW), BF16),
            sds((TOK, TOPK), jnp.int32),
            sds((TOK, TOPK), F32),
            sds(gate_up.shape[1:], BF16),
            sds(down.shape[1:], BF16),
        ),
        6,
        in_specs=[pl.BlockSpec(memory_space=pltpu.HBM)] * 6,
        scratch_shapes=small + [pltpu.SemaphoreType.DMA((6,))],
    )(
        *(
            pltpu.with_memory_space_constraint(v, pltpu.HBM)
            for v in (expert_ids.T, gate_values.T, tokens, out_grad, gate_up[0], down[0])
        )
    )
    arrived = lax.all_to_all(
        send.reshape(E, PAIR, DW), "expert", 0, 0, tiled=True
    ).reshape(SEND, DW)
    away, x, g = call(away_kernel, (wide16, narrow16, narrow16), 3, **work)(arrived, wgu, wd)
    got = lax.ppermute(away, "dp", SWAP)
    home = call(home_kernel, wide32, 4, **work)(x, g, wgu, wd)
    chip, own = call(add_kernel, (wide16, chunk32), 2)(home, got)
    got = lax.all_to_all(
        chip.reshape(RING, RX, 3 * H), "dp", 0, 0, axis_index_groups=FIRST, tiled=True
    )
    chunk, rest = call(sum_kernel, (chunk16, chunk32), 2)(got, own)
    parts = lax.all_gather(chunk, "dp", axis=0, axis_index_groups=SECOND)
    act = call(act_kernel, chunk16, 2)(parts, rest)
    mine = lax.all_gather(act, "dp", axis=0, axis_index_groups=FIRST, tiled=True)
    other = lax.ppermute(mine, "dp", SWAP)
    out, back = call(first_kernel, (narrow32, narrow32), 3, **work)(mine, wgu, wd)
    back = call(finish_kernel, sds((SEND, DW), BF16), 5)(other, wgu, wd, out, back)
    returned = lax.all_to_all(
        back.reshape(E, PAIR, DW), "expert", 0, 0, tiled=True
    ).reshape(SEND, DW)
    shape = sds((TOK, DW), BF16)
    return call(combine_kernel, (shape, shape), 3)(returned, weight, place)


def solution(mesh):
    rows, cols = P("expert", "dp"), P("expert", None)
    return jax.shard_map(
        local,
        mesh=mesh,
        in_specs=(rows, P("expert", "dp", None), P("expert", None, "dp"), cols, cols, rows),
        out_specs=(rows, rows),
        check_vma=False,
    )
```

time: 137 us -> 99.6 us (0.73)
  waiting for transfers between devices: 27.6 us -> 3.71 us
  between operations: 14.1 us -> 0.69 us
  local copies, waits for them, and re-layouts: 7.32 us -> 0 us
  starting transfers between devices: 2.09 us -> 6.91 us
  blocking collectives: 79.5 us -> 81.7 us
    all_gather x1 -> x0, waiting for transfers between devices: 24.9 us -> none  [local(): acts = lax.all_gather(act, ('x', 'c'), axis=0)]
    all_gather x1 -> x2, blocking collectives: 22.6 us -> 33.3 us  [the longest x1 19.5 us: local(): parts = lax.all_gather(chunk, 'dp', axis=0, axis_index_groups=SECOND)]
    all_to_all x3, blocking collectives: 56.9 us -> 48.4 us  [the longest x1 20.1 us: local(): lax.all_to_all(send.reshape(E, PAIR, DW), 'expert', 0, 0, tiled=True)]
    unnamed x16 -> x0, local copies, waits for them, and re-layouts: 7.32 us -> none
    ppermute x1 -> x2, starting transfers between devices: 2.05 us -> 6.91 us  [the longest x1 4.99 us: local(): other = lax.ppermute(mine, 'dp', SWAP)]
    pallas_call x6 -> x8, Pallas kernels: 4.66 us -> 6.01 us  [the longest x1 1.86 us: local(): call(pack_kernel, (sds((SEND, DW), BF16), sds((TOK, TOPK), jnp.int32), sd...]
    ppermute x1 -> x2, waiting for transfers between devices: 2.6 us -> 3.71 us  [the longest x1 2.05 us: local(): got = lax.ppermute(away, 'dp', SWAP)]
  transfers between devices with their start and end apart: 2 -> 2, of which waited for: 2 -> 2; matrix products, arithmetic and copies ran while one was open for 0% -> 0% of each run, Pallas kernels for 0% -> 1%
where the time goes in v2:
time: 99.6 us; the launch traced here: 99.3 us
  blocking collectives  81.7 us (82%)
  starting transfers between devices  6.91 us (7%)
  Pallas kernels  6.25 us (6%)
  waiting for transfers between devices  3.71 us (4%)
    all_to_all x1, blocking collectives, local(): lax.all_to_all(send.reshape(E, PAIR, DW), 'expert', 0, 0, tiled=True)  20.1 us
    all_gather x1, blocking collectives, local(): parts = lax.all_gather(chunk, 'dp', axis=0, axis_index_groups=SECOND)  19.5 us
    all_to_all x1, blocking collectives, local(): lax.all_to_all(chip.reshape(RING, RX, 3 * H), 'dp', 0, 0, axis_index_grou...  14.9 us
    all_gather x1, blocking collectives, local(): lax.all_gather(act, 'dp', axis=0, axis_index_groups=FIRST, tiled=True)  13.8 us
    all_to_all x1, blocking collectives, local(): lax.all_to_all(back.reshape(E, PAIR, DW), 'expert', 0, 0, tiled=True)  13.4 us
    ppermute x1, starting transfers between devices, local(): other = lax.ppermute(mine, 'dp', SWAP)  4.99 us
    ppermute x1, waiting for transfers between devices, local(): got = lax.ppermute(away, 'dp', SWAP)  2.05 us
  transfers between devices with their start and end apart: 2, of which 2 were waited for; matrix products, arithmetic and copies ran while one was open for 0% of the time, Pallas kernels for 1%

profile of v2, /device:TPU:8, one launch (start us, length us, event | category | flops | bytes accessed | tf_op | source)
XLA Modules:
  0.0 99.3 jit_solution(2789472191921540218)
XLA Ops:
  0.6 1.9 %shard_map.77 = (bf16[384,256]{1,0:T(8,128)(2,1)S(1)}, s32[64,2]{1,0:T(8,128)S(1)}, f32[64,2]{1,0:T(8,128)S(1)}, bf16[256,3584]{1,0:T(8,128)(2,1)S(1)}, bf16[1792,256]{1,0:T(8,128)(2,1)S(1)}) custom-call(s32[2,64]{1,0:T(2,128)} %bitcast.18, f32[2,64]{1,0:T(2,128)} %bitcast.19, bf16[64,256]{1,0:T(8,128)(2,1)} %tok_hbm.1, bf16[64,256]{1,0:T(8,128)(2,1)} %grad_hbm.1, ...), custom_call_target="tpu_custom_call" | custom-call | tf_op jit(solution)/shard_map/pallas_call | solution.py:215
  2.5 20.1 %all_to_all.15 = bf16[16,24,256]{2,1,0:T(8,128)(2,1)S(1)} all-to-all(bf16[16,24,256]{2,1,0:T(8,128)(2,1)S(1)} %bitcast.15), channel_id=1, replica_groups=mesh['dp'=32,'expert'=16] {'expert'}, dimensions={0} | all-to-all | bytes 393216 | tf_op jit(solution)/shard_map/all_to_all | solution.py:233
  22.6 0.7 shard_map.78
  23.3 1.9 %collective-permute-start = (bf16[192,2688]{1,0:T(8,128)(2,1)S(1)}, bf16[192,2688]{1,0:T(8,128)(2,1)S(1)}, u32[]{:S(2)}, u32[]{:S(2)}) collective-permute-start(bf16[192,2688]{1,0:T(8,128)(2,1)S(1)} %get-tuple-element.21), channel_id=1, source_target_pairs={{0,16},{16,0},{32,48},{48,32},{64,80},{80,64},{96,112},{112,96},{1... | collective-permute-start | bytes 3096584 | tf_op jit(solution)/shard_map/ppermute | solution.py:237
  25.2 0.5 shard_map.79.home_ref
  25.8 2.1 %collective-permute-done.got_ref = bf16[192,2688]{1,0:T(8,128)(2,1)S(1)} collective-permute-done((bf16[192,2688]{1,0:T(8,128)(2,1)S(1)}, bf16[192,2688]{1,0:T(8,128)(2,1)S(1)}, u32[]{:S(2)}, u32[]{:S(2)}) %collective-permute-start) | collective-permute-done | bytes 1032224 | tf_op jit(solution)/shard_map/ppermute | solution.py:237
  27.8 0.2 shard_map.80
  28.0 14.9 %all_to_all.16.got_ref = bf16[4,48,2688]{2,1,0:T(8,128)(2,1)S(1)} all-to-all(bf16[4,48,2688]{2,1,0:T(8,128)(2,1)S(1)} %bitcast.11), channel_id=1, replica_groups={{0,128,256,384},{32,160,288,416},{64,192,320,448},{96,224,352,480},{16,..., dimensions={0} | all-to-all | bytes 2064384 | tf_op jit(solution)/shard_map/all_to_all | solution.py:240
  42.9 0.3 shard_map.81
  43.2 19.5 %all-gather = bf16[192,2688]{1,0:T(8,128)(2,1)S(1)} all-gather(bf16[48,2688]{1,0:T(8,128)(2,1)S(1)} %get-tuple-element.24), channel_id=2, replica_groups={{0,32,64,96},{128,160,192,224},{256,288,320,352},{384,416,448,480},{16,..., dimensions={0}, use_global_device_ids=true | all-gather | bytes 1290240 | tf_op jit(solution)/shard_map/all_gather | solution.py:244
  62.8 0.2 shard_map.82
  63.0 13.8 %all_gather.11.act_ref = bf16[192,2688]{1,0:T(8,128)(2,1)S(1)} all-gather(bf16[48,2688]{1,0:T(8,128)(2,1)S(1)} %shard_map.82), channel_id=1, replica_groups={{0,128,256,384},{32,160,288,416},{64,192,320,448},{96,224,352,480},{16,..., dimensions={0}, use_global_device_ids=true | all-gather | bytes 1290240 | tf_op jit(solution)/shard_map/all_gather | solution.py:246
  76.8 5.0 %collective-permute-start.1 = (bf16[192,2688]{1,0:T(8,128)(2,1)S(1)}, bf16[192,2688]{1,0:T(8,128)(2,1)S(1)}, u32[]{:S(2)}, u32[]{:S(2)}) collective-permute-start(bf16[192,2688]{1,0:T(8,128)(2,1)S(1)} %all_gather.11.act_ref), channel_id=1, source_target_pairs={{0,16},{16,0},{32,48},{48,32},{64,80},{80,64},{96,112},{112,96},{1... | collective-permute-start | bytes 3096584 | tf_op jit(solution)/shard_map/ppermute | solution.py:247
  81.8 0.6 shard_map.83
  82.4 1.7 %collective-permute-done.1.act_ref = bf16[192,2688]{1,0:T(8,128)(2,1)S(1)} collective-permute-done((bf16[192,2688]{1,0:T(8,128)(2,1)S(1)}, bf16[192,2688]{1,0:T(8,128)(2,1)S(1)}, u32[]{:S(2)}, u32[]{:S(2)}) %collective-permute-start.1) | collective-permute-done | bytes 1032224 | tf_op jit(solution)/shard_map/ppermute | solution.py:247
  84.0 1.0 shard_map.84
  85.0 13.4 %all_to_all.17 = bf16[16,24,256]{2,1,0:T(8,128)(2,1)S(1)} all-to-all(bf16[16,24,256]{2,1,0:T(8,128)(2,1)S(1)} %bitcast.12), channel_id=1, replica_groups=mesh['dp'=32,'expert'=16] {'expert'}, dimensions={0} | all-to-all | bytes 393216 | tf_op jit(solution)/shard_map/all_to_all | solution.py:250
  98.4 0.9 shard_map.85
Async XLA Ops:
  23.3 4.5 %collective-permute-start = (bf16[192,2688]{1,0:T(8,128)(2,1)S(1)}, bf16[192,2688]{1,0:T(8,128)(2,1)S(1)}, u32[]{:S(2)}, u32[]{:S(2)}) collective-permute-start(bf16[192,2688]{1,0:T(8,128)(2,1)S(1)} %get-tuple-element.21), channel_id=1, source_target_pairs={{0,16},{16,0},{32,48},{48,32},{64,80},{80,64},{96,112},{112,96},{1... | collective-permute-start | bytes 3096584 | tf_op jit(solution)/shard_map/ppermute | solution.py:237
  76.8 7.2 %collective-permute-start.1 = (bf16[192,2688]{1,0:T(8,128)(2,1)S(1)}, bf16[192,2688]{1,0:T(8,128)(2,1)S(1)}, u32[]{:S(2)}, u32[]{:S(2)}) collective-permute-start(bf16[192,2688]{1,0:T(8,128)(2,1)S(1)} %all_gather.11.act_ref), channel_id=1, source_target_pairs={{0,16},{16,0},{32,48},{48,32},{64,80},{80,64},{96,112},{112,96},{1... | collective-permute-start | bytes 3096584 | tf_op jit(solution)/shard_map/ppermute | solution.py:247

commit v3 on v2

--- a/solution.py
+++ b/solution.py
@@ -69,14 +69,27 @@
     return jnp.sum(jnp.where(eye, row, jnp.zeros_like(row)), axis=1, keepdims=True)
 
 
+def half_columns(c):
+    return pl.ds(pl.multiple_of(c * H, H), H), pl.ds(pl.multiple_of(F + c * H, H), H)
+
+
+def fetch_half(wgu_hbm, wd_hbm, wgu_ref, wd_ref, sems, c):
+    gate, up = half_columns(c)
+    return [
+        pltpu.make_async_copy(wgu_hbm.at[:, gate], wgu_ref.at[:, pl.ds(0, H)], sems.at[0]),
+        pltpu.make_async_copy(wgu_hbm.at[:, up], wgu_ref.at[:, pl.ds(H, H)], sems.at[1]),
+        pltpu.make_async_copy(wd_hbm.at[gate, :], wd_ref, sems.at[2]),
+    ]
+
+
 def pack_kernel(
     ids_hbm, gate_hbm, tok_hbm, grad_hbm, wgu_hbm, wd_hbm,
     send_ref, place_ref, weight_ref, wgu_out, wd_out,
-    ids_ref, gate_ref, tok_ref, grad_ref, sems,
+    ids_ref, gate_ref, tok_ref, grad_ref, sems, half_sems,
 ):
     pairs = [(ids_hbm, ids_ref), (gate_hbm, gate_ref), (tok_hbm, tok_ref), (grad_hbm, grad_ref)]
-    pairs += [(wgu_hbm, wgu_out), (wd_hbm, wd_out)]
     moves = [pltpu.make_async_copy(*pair, sems.at[n]) for n, pair in enumerate(pairs)]
+    moves += fetch_half(wgu_hbm, wd_hbm, wgu_out, wd_out, half_sems, 1 - core())
     for move in moves:
         move.start()
     eye = iota((TOK, TOK), 0) == iota((TOK, TOK), 1)
@@ -115,13 +128,8 @@
     return slot + extra
 
 
-def half_columns(c):
-    return pl.ds(pl.multiple_of(c * H, H), H), pl.ds(pl.multiple_of(F + c * H, H), H)
-
-
-def partials(x, g, wgu_ref, wd_ref, c):
-    gate, up = half_columns(c)
-    return mm(x, wgu_ref[:, gate]), mm(x, wgu_ref[:, up]), mm_t(g, wd_ref[gate, :])
+def partials(x, g, wgu_ref, wd_ref):
+    return mm(x, wgu_ref[:, :H]), mm(x, wgu_ref[:, H:]), mm_t(g, wd_ref[...])
 
 
 def away_kernel(arr_ref, wgu_ref, wd_ref, out_ref, x_ref, g_ref):
@@ -130,13 +138,18 @@
     col = iota((ROWS, SEND), 1)
     x_ref[...] = mm(onehot(col == source), arrived).astype(BF16)
     g_ref[...] = mm(onehot(col == source + CAP), arrived).astype(BF16)
-    terms = partials(x_ref[...], g_ref[...], wgu_ref, wd_ref, 1 - core())
+    terms = partials(x_ref[...], g_ref[...], wgu_ref, wd_ref)
     for j, term in enumerate(terms):
         out_ref[:, j * H : (j + 1) * H] = term.astype(BF16)
 
 
-def home_kernel(x_ref, g_ref, wgu_ref, wd_ref, out_ref):
-    terms = partials(x_ref[...], g_ref[...], wgu_ref, wd_ref, core())
+def home_kernel(x_ref, g_ref, wgu_hbm, wd_hbm, out_ref, wgu_out, wd_out, half_sems):
+    moves = fetch_half(wgu_hbm, wd_hbm, wgu_out, wd_out, half_sems, core())
+    for move in moves:
+        move.start()
+    for move in moves:
+        move.wait()
+    terms = partials(x_ref[...], g_ref[...], wgu_out, wd_out)
     for j, term in enumerate(terms):
         out_ref[:, j * H : (j + 1) * H] = term
 
@@ -153,7 +166,7 @@
     for j in range(RING):
         total += got_ref[j].astype(F32)
     rounded = total.astype(BF16)
-    out_ref[...] = rounded
+    out_ref[0] = rounded
     rest_ref[...] = total - rounded.astype(F32)
 
 
@@ -164,94 +177,106 @@
     gate, up, hg = total[:, :H], total[:, H : 2 * H], total[:, 2 * H :]
     sig = jax.nn.sigmoid(gate)
     silu = gate * sig
-    out_ref[:, :H] = (silu * up).astype(BF16)
-    out_ref[:, H : 2 * H] = (hg * up * sig * (1.0 + gate * (1.0 - sig))).astype(BF16)
-    out_ref[:, 2 * H :] = (hg * silu).astype(BF16)
-
-
-def products(act_ref, wgu_ref, wd_ref, c):
-    gate, up = half_columns(c)
-    out = mm(act_ref[:, :H], wd_ref[gate, :])
-    back = mm_t(act_ref[:, H : 2 * H], wgu_ref[:, gate])
-    return out, back + mm_t(act_ref[:, 2 * H :], wgu_ref[:, up])
-
-
-def first_kernel(act_ref, wgu_ref, wd_ref, out_ref, back_ref):
-    out_ref[...], back_ref[...] = products(act_ref, wgu_ref, wd_ref, core())
-
-
-def finish_kernel(act_ref, wgu_ref, wd_ref, out_ref, back_ref, send_ref):
-    out, back = products(act_ref, wgu_ref, wd_ref, 1 - core())
+    out_ref[0, :, :H] = (silu * up).astype(BF16)
+    out_ref[0, :, H : 2 * H] = (hg * up * sig * (1.0 + gate * (1.0 - sig))).astype(BF16)
+    out_ref[0, :, 2 * H :] = (hg * silu).astype(BF16)
+
+
+def products(act_ref, wgu_ref, wd_ref):
+    back = mm_t(act_ref[:, H : 2 * H], wgu_ref[:, :H]) + mm_t(act_ref[:, 2 * H :], wgu_ref[:, H:])
+    return mm(act_ref[:, :H], wd_ref[...]), back
+
+
+def first_kernel(act_ref, wgu_ref, wd_ref, place_ref, out_ref, back_ref, spread_ref, pick_ref):
+    out_ref[...], back_ref[...] = products(act_ref, wgu_ref, wd_ref)
     row = iota((SEND, ROWS), 0)
     target = slot_to_pair(iota((1, ROWS), 1))
-    send = mm(onehot(row == target), (out_ref[...] + out).astype(BF16))
-    send += mm(onehot(row == target + CAP), (back_ref[...] + back).astype(BF16))
-    send_ref[...] = send.astype(BF16)
-
-
-def combine_kernel(ret_ref, weight_ref, place_ref, moe_ref, tok_ref):
-    returned = ret_ref[...]
+    spread_ref[:, :ROWS] = onehot(row == target)
+    spread_ref[:, ROWS:] = onehot(row == target + CAP)
     col = iota((TOK, SEND), 1)
-    place = place_ref[...]
-    moe = jnp.zeros((TOK, DW), F32)
-    pick = jnp.zeros((TOK, SEND), BF16)
+    at = [place_ref[:, k : k + 1] for k in range(TOPK)]
     for k in range(TOPK):
-        at = place[:, k : k + 1]
-        moe += weight_ref[:, k : k + 1] * mm(onehot(col == at), returned)
-        pick += onehot(col == at + CAP)
+        pick_ref[k * TOK : (k + 1) * TOK, :] = onehot(col == at[k])
+    pick_ref[TOPK * TOK :, :] = onehot((col == at[0] + CAP) | (col == at[1] + CAP))
+
+
+def finish_kernel(act_ref, wgu_ref, wd_ref, out_ref, back_ref, spread_ref, send_ref):
+    out, back = products(act_ref, wgu_ref, wd_ref)
+    rows = [(out_ref[...] + out).astype(BF16), (back_ref[...] + back).astype(BF16)]
+    send_ref[...] = mm(spread_ref[...], jnp.concatenate(rows, axis=0)).astype(BF16)
+
+
+def combine_kernel(ret_ref, weight_ref, pick_ref, moe_ref, tok_ref):
+    picked = mm(pick_ref[...], ret_ref[...])
+    moe = weight_ref[:, :1] * picked[:TOK]
+    for k in range(1, TOPK):
+        moe += weight_ref[:, k : k + 1] * picked[k * TOK : (k + 1) * TOK]
     moe_ref[...] = moe.astype(BF16)
-    tok_ref[...] = mm(pick, returned).astype(BF16)
+    tok_ref[...] = picked[TOPK * TOK :].astype(BF16)
 
 
 def local(tokens, gate_up, down, expert_ids, gate_values, out_grad):
     sds = jax.ShapeDtypeStruct
     wide16, wide32 = (sds((ROWS, 3 * H), t) for t in (BF16, F32))
     narrow16, narrow32 = (sds((ROWS, DW), t) for t in (BF16, F32))
-    chunk16, chunk32 = (sds((RX, 3 * H), t) for t in (BF16, F32))
+    chunk16, chunk32 = sds((1, RX, 3 * H), BF16), sds((RX, 3 * H), F32)
     small = [pltpu.VMEM((TOPK, TOK), jnp.int32), pltpu.VMEM((TOPK, TOK), F32)]
     small += [pltpu.VMEM((TOK, DW), BF16)] * 2
+    half = (sds((DW, 2 * H), BF16), sds((H, DW), BF16))
+    hbm = pl.BlockSpec(memory_space=pltpu.HBM)
+    in_hbm = lambda *vs: [pltpu.with_memory_space_constraint(v, pltpu.HBM) for v in vs]
+    wgu, wd = in_hbm(gate_up[0], down[0])
     work = dict(flops=2 * ROWS * DW * 3 * H, nbytes=4 << 20)
 
-    send, place, weight, wgu, wd = call(
+    send, place, weight, wgu_away, wd_away = call(
         pack_kernel,
         (
             sds((SEND, DW), BF16),
             sds((TOK, TOPK), jnp.int32),
             sds((TOK, TOPK), F32),
-            sds(gate_up.shape[1:], BF16),
-            sds(down.shape[1:], BF16),
+            *half,
         ),
         6,
-        in_specs=[pl.BlockSpec(memory_space=pltpu.HBM)] * 6,
-        scratch_shapes=small + [pltpu.SemaphoreType.DMA((6,))],
-    )(
-        *(
-            pltpu.with_memory_space_constraint(v, pltpu.HBM)
-            for v in (expert_ids.T, gate_values.T, tokens, out_grad, gate_up[0], down[0])
-        )
-    )
+        in_specs=[hbm] * 6,
+        scratch_shapes=small + [pltpu.SemaphoreType.DMA((n,)) for n in (4, 3)],
+    )(*in_hbm(expert_ids.T, gate_values.T, tokens, out_grad), wgu, wd)
     arrived = lax.all_to_all(
         send.reshape(E, PAIR, DW), "expert", 0, 0, tiled=True
     ).reshape(SEND, DW)
-    away, x, g = call(away_kernel, (wide16, narrow16, narrow16), 3, **work)(arrived, wgu, wd)
+    away, x, g = call(away_kernel, (wide16, narrow16, narrow16), 3, **work)(
+        arrived, wgu_away, wd_away
+    )
     got = lax.ppermute(away, "dp", SWAP)
-    home = call(home_kernel, wide32, 4, **work)(x, g, wgu, wd)
+    home, wgu_home, wd_home = call(
+        home_kernel,
+        (wide32, *half),
+        4,
+        in_specs=[VMEM, VMEM, hbm, hbm],
+        scratch_shapes=[pltpu.SemaphoreType.DMA((3,))],
+        **work,
+    )(x, g, wgu, wd)
     chip, own = call(add_kernel, (wide16, chunk32), 2)(home, got)
     got = lax.all_to_all(
         chip.reshape(RING, RX, 3 * H), "dp", 0, 0, axis_index_groups=FIRST, tiled=True
     )
     chunk, rest = call(sum_kernel, (chunk16, chunk32), 2)(got, own)
-    parts = lax.all_gather(chunk, "dp", axis=0, axis_index_groups=SECOND)
+    parts = lax.all_gather(chunk, "dp", axis=0, axis_index_groups=SECOND, tiled=True)
     act = call(act_kernel, chunk16, 2)(parts, rest)
     mine = lax.all_gather(act, "dp", axis=0, axis_index_groups=FIRST, tiled=True)
+    mine = mine.reshape(ROWS, 3 * H)
     other = lax.ppermute(mine, "dp", SWAP)
-    out, back = call(first_kernel, (narrow32, narrow32), 3, **work)(mine, wgu, wd)
-    back = call(finish_kernel, sds((SEND, DW), BF16), 5)(other, wgu, wd, out, back)
+    spread, pick = sds((SEND, 2 * ROWS), BF16), sds(((TOPK + 1) * TOK, SEND), BF16)
+    out, back, spread, pick = call(first_kernel, (narrow32, narrow32, spread, pick), 4, **work)(
+        mine, wgu_home, wd_home, place
+    )
+    back = call(finish_kernel, sds((SEND, DW), BF16), 6)(
+        other, wgu_away, wd_away, out, back, spread
+    )
     returned = lax.all_to_all(
         back.reshape(E, PAIR, DW), "expert", 0, 0, tiled=True
     ).reshape(SEND, DW)
     shape = sds((TOK, DW), BF16)
-    return call(combine_kernel, (shape, shape), 3)(returned, weight, place)
+    return call(combine_kernel, (shape, shape), 3)(returned, weight, pick)
 
 
 def solution(mesh):

time: 99.6 us -> 99.3 us (level)
  waiting for transfers between devices: 3.71 us -> 2.36 us
    ppermute x1, waiting for transfers between devices: 2.05 us -> 0.73 us  [local(): got = lax.ppermute(away, 'dp', SWAP)]
    pallas_call x5, Pallas kernels: 3.69 us -> 4.94 us  [the longest x1 1.87 us: local(): call(home_kernel, (wide32, *half), 4, in_specs=[VMEM, VMEM, hbm, hbm], sc...]
  transfers between devices with their start and end apart: 2 -> 2, of which waited for: 2 -> 2; matrix products, arithmetic and copies ran while one was open for 0% -> 0% of each run, Pallas kernels for 1% -> 2%
where the time goes in v3:
time: 99.3 us; the launch traced here: 99 us
  blocking collectives  81.9 us (82%)
  Pallas kernels  7.14 us (7%)
  starting transfers between devices  6.87 us (7%)
  waiting for transfers between devices  2.36 us (2%)
    all_to_all x1, blocking collectives, local(): lax.all_to_all(send.reshape(E, PAIR, DW), 'expert', 0, 0, tiled=True)  20.1 us
    all_gather x1, blocking collectives, local(): lax.all_gather(chunk, 'dp', axis=0, axis_index_groups=SECOND, tiled=True)  19.7 us
    all_to_all x1, blocking collectives, local(): lax.all_to_all(chip.reshape(RING, RX, 3 * H), 'dp', 0, 0, axis_index_grou...  14.9 us
    all_gather x1, blocking collectives, local(): lax.all_gather(act, 'dp', axis=0, axis_index_groups=FIRST, tiled=True)  13.8 us
    all_to_all x1, blocking collectives, local(): lax.all_to_all(back.reshape(E, PAIR, DW), 'expert', 0, 0, tiled=True)  13.4 us
    ppermute x1, starting transfers between devices, local(): other = lax.ppermute(mine, 'dp', SWAP)  4.95 us
  transfers between devices with their start and end apart: 2, of which 2 were waited for; matrix products, arithmetic and copies ran while one was open for 0% of the time, Pallas kernels for 2%

profile of v3, /device:TPU:8, one launch (start us, length us, event | category | flops | bytes accessed | tf_op | source)
XLA Modules:
  0.0 99.0 jit_solution(16800171243369439577)
XLA Ops:
  0.6 1.4 %shard_map.77 = (bf16[384,256]{1,0:T(8,128)(2,1)S(1)}, s32[64,2]{1,0:T(8,128)S(1)}, f32[64,2]{1,0:T(8,128)S(1)}, bf16[256,1792]{1,0:T(8,128)(2,1)S(1)}, bf16[896,256]{1,0:T(8,128)(2,1)S(1)}) custom-call(s32[2,64]{1,0:T(2,128)} %bitcast.21, f32[2,64]{1,0:T(2,128)} %bitcast.22, bf16[64,256]{1,0:T(8,128)(2,1)} %tok_hbm.1, bf16[64,256]{1,0:T(8,128)(2,1)} %grad_hbm.1, ...), custom_call_target="tpu_custom_call" | custom-call | tf_op jit(solution)/shard_map/pallas_call | solution.py:231
  2.1 20.1 %all_to_all.15 = bf16[16,24,256]{2,1,0:T(8,128)(2,1)S(1)} all-to-all(bf16[16,24,256]{2,1,0:T(8,128)(2,1)S(1)} %bitcast.16), channel_id=1, replica_groups=mesh['dp'=32,'expert'=16] {'expert'}, dimensions={0} | all-to-all | bytes 393216 | tf_op jit(solution)/shard_map/all_to_all | solution.py:243
  22.1 0.7 shard_map.78
  22.9 1.9 %collective-permute-start = (bf16[192,2688]{1,0:T(8,128)(2,1)S(1)}, bf16[192,2688]{1,0:T(8,128)(2,1)S(1)}, u32[]{:S(2)}, u32[]{:S(2)}) collective-permute-start(bf16[192,2688]{1,0:T(8,128)(2,1)S(1)} %get-tuple-element.27), channel_id=1, source_target_pairs={{0,16},{16,0},{32,48},{48,32},{64,80},{80,64},{96,112},{112,96},{1... | collective-permute-start | bytes 3096584 | tf_op jit(solution)/shard_map/ppermute | solution.py:249
  24.8 1.9 %shard_map.79 = (f32[192,2688]{1,0:T(8,128)S(1)}, bf16[256,1792]{1,0:T(8,128)(2,1)S(1)}, bf16[896,256]{1,0:T(8,128)(2,1)S(1)}) custom-call(bf16[192,256]{1,0:T(8,128)(2,1)S(1)} %get-tuple-element.24.x_ref, bf16[192,256]{1,0:T(8,128)(2,1)S(1)} %get-tuple-element.25.g_ref, bf16[256,3584]{1,0:T(8,128)(2,1)} %bitcast.18, bf16[1792,256]{1,0:T(8,128)(2,1)} %bitcast.20), custom_call_target="tpu_custom_call" | custom-call | flops 264241152 | bytes 4194304 | tf_op jit(solution)/shard_map/pallas_call | solution.py:250
  26.7 0.7 collective-permute-done.got_ref
  27.4 0.3 shard_map.80
  27.7 14.9 %all_to_all.16.got_ref = bf16[4,48,2688]{2,1,0:T(8,128)(2,1)S(1)} all-to-all(bf16[4,48,2688]{2,1,0:T(8,128)(2,1)S(1)} %bitcast.12), channel_id=1, replica_groups={{0,128,256,384},{32,160,288,416},{64,192,320,448},{96,224,352,480},{16,..., dimensions={0} | all-to-all | bytes 2064384 | tf_op jit(solution)/shard_map/all_to_all | solution.py:259
  42.6 0.2 shard_map.81
  42.8 19.7 %all_gather.6.part_ref = bf16[4,48,2688]{2,1,0:T(8,128)(2,1)S(1)} all-gather(bf16[1,48,2688]{2,1,0:T(8,128)(2,1)S(1)} %get-tuple-element.30), channel_id=1, replica_groups={{0,32,64,96},{128,160,192,224},{256,288,320,352},{384,416,448,480},{16,..., dimensions={0}, use_global_device_ids=true | all-gather | bytes 1290240 | tf_op jit(solution)/shard_map/all_gather | solution.py:263
  62.5 0.2 shard_map.82
  62.8 13.8 %all_gather.7 = bf16[4,48,2688]{2,1,0:T(8,128)(2,1)S(1)} all-gather(bf16[1,48,2688]{2,1,0:T(8,128)(2,1)S(1)} %shard_map.82), channel_id=1, replica_groups={{0,128,256,384},{32,160,288,416},{64,192,320,448},{96,224,352,480},{16,..., dimensions={0}, use_global_device_ids=true | all-gather | bytes 1290240 | tf_op jit(solution)/shard_map/all_gather | solution.py:265
  76.6 4.9 %collective-permute-start.1 = (bf16[192,2688]{1,0:T(8,128)(2,1)S(1)}, bf16[192,2688]{1,0:T(8,128)(2,1)S(1)}, u32[]{:S(2)}, u32[]{:S(2)}) collective-permute-start(bf16[192,2688]{1,0:T(8,128)(2,1)S(1)} %bitcast.10), channel_id=1, source_target_pairs={{0,16},{16,0},{32,48},{48,32},{64,80},{80,64},{96,112},{112,96},{1... | collective-permute-start | bytes 3096584 | tf_op jit(solution)/shard_map/ppermute | solution.py:267
  81.5 0.6 shard_map.83
  82.1 1.6 %collective-permute-done.1.act_ref = bf16[192,2688]{1,0:T(8,128)(2,1)S(1)} collective-permute-done((bf16[192,2688]{1,0:T(8,128)(2,1)S(1)}, bf16[192,2688]{1,0:T(8,128)(2,1)S(1)}, u32[]{:S(2)}, u32[]{:S(2)}) %collective-permute-start.1) | collective-permute-done | bytes 1032224 | tf_op jit(solution)/shard_map/ppermute | solution.py:267
  83.8 0.9 shard_map.84
  84.7 13.4 %all_to_all.17 = bf16[16,24,256]{2,1,0:T(8,128)(2,1)S(1)} all-to-all(bf16[16,24,256]{2,1,0:T(8,128)(2,1)S(1)} %bitcast.13), channel_id=1, replica_groups=mesh['dp'=32,'expert'=16] {'expert'}, dimensions={0} | all-to-all | bytes 393216 | tf_op jit(solution)/shard_map/all_to_all | solution.py:275
  98.1 0.8 shard_map.85
Async XLA Ops:
  22.9 4.5 %collective-permute-start = (bf16[192,2688]{1,0:T(8,128)(2,1)S(1)}, bf16[192,2688]{1,0:T(8,128)(2,1)S(1)}, u32[]{:S(2)}, u32[]{:S(2)}) collective-permute-start(bf16[192,2688]{1,0:T(8,128)(2,1)S(1)} %get-tuple-element.27), channel_id=1, source_target_pairs={{0,16},{16,0},{32,48},{48,32},{64,80},{80,64},{96,112},{112,96},{1... | collective-permute-start | bytes 3096584 | tf_op jit(solution)/shard_map/ppermute | solution.py:249
  76.6 7.2 %collective-permute-start.1 = (bf16[192,2688]{1,0:T(8,128)(2,1)S(1)}, bf16[192,2688]{1,0:T(8,128)(2,1)S(1)}, u32[]{:S(2)}, u32[]{:S(2)}) collective-permute-start(bf16[192,2688]{1,0:T(8,128)(2,1)S(1)} %bitcast.10), channel_id=1, source_target_pairs={{0,16},{16,0},{32,48},{48,32},{64,80},{80,64},{96,112},{112,96},{1... | collective-permute-start | bytes 3096584 | tf_op jit(solution)/shard_map/ppermute | solution.py:267

commit v4 on v3

--- a/solution.py
+++ b/solution.py
@@ -94,7 +94,6 @@
         move.start()
     eye = iota((TOK, TOK), 0) == iota((TOK, TOK), 1)
     before = onehot(iota((TOK, TOK), 0) < iota((TOK, TOK), 1))
-    row = iota((SEND, TOK), 0)
     moves[0].wait()
     moves[1].wait()
     ids = ids_ref[...]
@@ -110,34 +109,30 @@
     place_ref[...] = jnp.concatenate(places, axis=1)
     weight_ref[...] = jnp.concatenate(weights, axis=1)
     moves[2].wait()
-    pick_tok = onehot((row == across[0]) | (row == across[1]))
-    total = mm(pick_tok, tok_ref[...])
     moves[3].wait()
     grad = grad_ref[...].astype(F32)
-    for k in range(TOPK):
-        total += mm(onehot(row == across[k] + CAP), (weights[k] * grad).astype(BF16))
+    values = [tok_ref[...]] + [(weights[k] * grad).astype(BF16) for k in range(TOPK)]
+    first = jnp.concatenate(across[:1] + [at + CAP for at in across], axis=1)
+    second = jnp.concatenate(across[1:2] + [at + CAP for at in across], axis=1)
+    row = iota((SEND, TOK * (TOPK + 1)), 0)
+    pick = onehot((row == first) | (row == second))
+    total = mm(pick, jnp.concatenate(values, axis=0))
     send_ref[...] = total.astype(BF16)
     for move in moves[4:]:
         move.wait()
 
 
-def slot_to_pair(slot):
-    extra = jnp.zeros_like(slot)
-    for b in range(1, E):
-        extra += jnp.where(slot >= b * CAP, CAP, 0)
-    return slot + extra
-
-
 def partials(x, g, wgu_ref, wd_ref):
     return mm(x, wgu_ref[:, :H]), mm(x, wgu_ref[:, H:]), mm_t(g, wd_ref[...])
 
 
-def away_kernel(arr_ref, wgu_ref, wd_ref, out_ref, x_ref, g_ref):
-    arrived = arr_ref[...]
-    source = slot_to_pair(iota((ROWS, 1), 0))
-    col = iota((ROWS, SEND), 1)
-    x_ref[...] = mm(onehot(col == source), arrived).astype(BF16)
-    g_ref[...] = mm(onehot(col == source + CAP), arrived).astype(BF16)
+def away_kernel(arr_ref, wgu_ref, wd_ref, out_ref, x_ref, g_ref, pair_ref, sort_ref):
+    pair_ref[...] = arr_ref[...].astype(F32)
+    for n, rows_ref in enumerate((x_ref, g_ref)):
+        for b in range(E):
+            at = b * PAIR + n * CAP
+            sort_ref[b * CAP : (b + 1) * CAP, :] = pair_ref[at : at + CAP, :]
+        rows_ref[...] = sort_ref[...].astype(BF16)
     terms = partials(x_ref[...], g_ref[...], wgu_ref, wd_ref)
     for j, term in enumerate(terms):
         out_ref[:, j * H : (j + 1) * H] = term.astype(BF16)
@@ -187,12 +182,8 @@
     return mm(act_ref[:, :H], wd_ref[...]), back
 
 
-def first_kernel(act_ref, wgu_ref, wd_ref, place_ref, out_ref, back_ref, spread_ref, pick_ref):
+def first_kernel(act_ref, wgu_ref, wd_ref, place_ref, out_ref, back_ref, pick_ref):
     out_ref[...], back_ref[...] = products(act_ref, wgu_ref, wd_ref)
-    row = iota((SEND, ROWS), 0)
-    target = slot_to_pair(iota((1, ROWS), 1))
-    spread_ref[:, :ROWS] = onehot(row == target)
-    spread_ref[:, ROWS:] = onehot(row == target + CAP)
     col = iota((TOK, SEND), 1)
     at = [place_ref[:, k : k + 1] for k in range(TOPK)]
     for k in range(TOPK):
@@ -200,10 +191,14 @@
     pick_ref[TOPK * TOK :, :] = onehot((col == at[0] + CAP) | (col == at[1] + CAP))
 
 
-def finish_kernel(act_ref, wgu_ref, wd_ref, out_ref, back_ref, spread_ref, send_ref):
-    out, back = products(act_ref, wgu_ref, wd_ref)
-    rows = [(out_ref[...] + out).astype(BF16), (back_ref[...] + back).astype(BF16)]
-    send_ref[...] = mm(spread_ref[...], jnp.concatenate(rows, axis=0)).astype(BF16)
+def finish_kernel(act_ref, wgu_ref, wd_ref, out_ref, back_ref, send_ref, pair_ref, sort_ref):
+    terms = products(act_ref, wgu_ref, wd_ref)
+    for n, (own_ref, term) in enumerate(zip((out_ref, back_ref), terms)):
+        sort_ref[...] = own_ref[...] + term
+        for b in range(E):
+            at = b * PAIR + n * CAP
+            pair_ref[at : at + CAP, :] = sort_ref[b * CAP : (b + 1) * CAP, :]
+    send_ref[...] = pair_ref[...].astype(BF16)
 
 
 def combine_kernel(ret_ref, weight_ref, pick_ref, moe_ref, tok_ref):
@@ -243,7 +238,13 @@
     arrived = lax.all_to_all(
         send.reshape(E, PAIR, DW), "expert", 0, 0, tiled=True
     ).reshape(SEND, DW)
-    away, x, g = call(away_kernel, (wide16, narrow16, narrow16), 3, **work)(
+    away, x, g = call(
+        away_kernel,
+        (wide16, narrow16, narrow16),
+        3,
+        scratch_shapes=[pltpu.VMEM((SEND, DW), F32), pltpu.VMEM((ROWS, DW), F32)],
+        **work,
+    )(
         arrived, wgu_away, wd_away
     )
     got = lax.ppermute(away, "dp", SWAP)
@@ -265,13 +266,16 @@
     mine = lax.all_gather(act, "dp", axis=0, axis_index_groups=FIRST, tiled=True)
     mine = mine.reshape(ROWS, 3 * H)
     other = lax.ppermute(mine, "dp", SWAP)
-    spread, pick = sds((SEND, 2 * ROWS), BF16), sds(((TOPK + 1) * TOK, SEND), BF16)
-    out, back, spread, pick = call(first_kernel, (narrow32, narrow32, spread, pick), 4, **work)(
+    pick = sds(((TOPK + 1) * TOK, SEND), BF16)
+    out, back, pick = call(first_kernel, (narrow32, narrow32, pick), 4, **work)(
         mine, wgu_home, wd_home, place
     )
-    back = call(finish_kernel, sds((SEND, DW), BF16), 6)(
-        other, wgu_away, wd_away, out, back, spread
-    )
+    back = call(
+        finish_kernel,
+        sds((SEND, DW), BF16),
+        5,
+        scratch_shapes=[pltpu.VMEM((SEND, DW), F32), pltpu.VMEM((ROWS, DW), F32)],
+    )(other, wgu_away, wd_away, out, back)
     returned = lax.all_to_all(
         back.reshape(E, PAIR, DW), "expert", 0, 0, tiled=True
     ).reshape(SEND, DW)

time: 99.3 us -> 98.7 us (level)
  no operation moved by 1% of the time
where the time goes in v4:
time: 98.7 us; the launch traced here: 98.3 us
  blocking collectives  81 us (82%)
  starting transfers between devices  7.67 us (8%)
  Pallas kernels  6.6 us (7%)
  waiting for transfers between devices  2.39 us (2%)
    all_to_all x1, blocking collectives, local(): lax.all_to_all(send.reshape(E, PAIR, DW), 'expert', 0, 0, tiled=True)  20.1 us
    all_gather x1, blocking collectives, local(): lax.all_gather(chunk, 'dp', axis=0, axis_index_groups=SECOND, tiled=True)  19 us
    all_to_all x1, blocking collectives, local(): lax.all_to_all(chip.reshape(RING, RX, 3 * H), 'dp', 0, 0, axis_index_grou...  14.9 us
    all_gather x1, blocking collectives, local(): lax.all_gather(act, 'dp', axis=0, axis_index_groups=FIRST, tiled=True)  13.8 us
    all_to_all x1, blocking collectives, local(): lax.all_to_all(back.reshape(E, PAIR, DW), 'expert', 0, 0, tiled=True)  13.2 us
    ppermute x1, starting transfers between devices, local(): other = lax.ppermute(mine, 'dp', SWAP)  5.75 us
  transfers between devices with their start and end apart: 2, of which 2 were waited for; matrix products, arithmetic and copies ran while one was open for 0% of the time, Pallas kernels for 2%

profile of v4, /device:TPU:8, one launch (start us, length us, event | category | flops | bytes accessed | tf_op | source)
XLA Modules:
  0.0 98.3 jit_solution(15538966547798150665)
XLA Ops:
  0.6 1.4 %shard_map.77 = (bf16[384,256]{1,0:T(8,128)(2,1)S(1)}, s32[64,2]{1,0:T(8,128)S(1)}, f32[64,2]{1,0:T(8,128)S(1)}, bf16[256,1792]{1,0:T(8,128)(2,1)S(1)}, bf16[896,256]{1,0:T(8,128)(2,1)S(1)}) custom-call(s32[2,64]{1,0:T(2,128)} %bitcast.21, f32[2,64]{1,0:T(2,128)} %bitcast.22, bf16[64,256]{1,0:T(8,128)(2,1)} %tok_hbm.1, bf16[64,256]{1,0:T(8,128)(2,1)} %grad_hbm.1, ...), custom_call_target="tpu_custom_call" | custom-call | tf_op jit(solution)/shard_map/pallas_call | solution.py:226
  2.1 20.1 %all_to_all.15 = bf16[16,24,256]{2,1,0:T(8,128)(2,1)S(1)} all-to-all(bf16[16,24,256]{2,1,0:T(8,128)(2,1)S(1)} %bitcast.16), channel_id=1, replica_groups=mesh['dp'=32,'expert'=16] {'expert'}, dimensions={0} | all-to-all | bytes 393216 | tf_op jit(solution)/shard_map/all_to_all | solution.py:238
  22.1 0.5 shard_map.78
  22.7 1.9 %collective-permute-start = (bf16[192,2688]{1,0:T(8,128)(2,1)S(1)}, bf16[192,2688]{1,0:T(8,128)(2,1)S(1)}, u32[]{:S(2)}, u32[]{:S(2)}) collective-permute-start(bf16[192,2688]{1,0:T(8,128)(2,1)S(1)} %get-tuple-element.26), channel_id=1, source_target_pairs={{0,16},{16,0},{32,48},{48,32},{64,80},{80,64},{96,112},{112,96},{1... | collective-permute-start | bytes 3096584 | tf_op jit(solution)/shard_map/ppermute | solution.py:250
  24.6 1.9 %shard_map.79 = (f32[192,2688]{1,0:T(8,128)S(1)}, bf16[256,1792]{1,0:T(8,128)(2,1)S(1)}, bf16[896,256]{1,0:T(8,128)(2,1)S(1)}) custom-call(bf16[192,256]{1,0:T(8,128)(2,1)S(1)} %get-tuple-element.23.x_ref, bf16[192,256]{1,0:T(8,128)(2,1)S(1)} %get-tuple-element.24.g_ref, bf16[256,3584]{1,0:T(8,128)(2,1)} %bitcast.18, bf16[1792,256]{1,0:T(8,128)(2,1)} %bitcast.20), custom_call_target="tpu_custom_call" | custom-call | flops 264241152 | bytes 4194304 | tf_op jit(solution)/shard_map/pallas_call | solution.py:251
  26.5 0.7 collective-permute-done.got_ref
  27.2 0.3 shard_map.80
  27.5 14.9 %all_to_all.16.got_ref = bf16[4,48,2688]{2,1,0:T(8,128)(2,1)S(1)} all-to-all(bf16[4,48,2688]{2,1,0:T(8,128)(2,1)S(1)} %bitcast.12), channel_id=1, replica_groups={{0,128,256,384},{32,160,288,416},{64,192,320,448},{96,224,352,480},{16,..., dimensions={0} | all-to-all | bytes 2064384 | tf_op jit(solution)/shard_map/all_to_all | solution.py:260
  42.4 0.2 shard_map.81
  42.6 19.0 %all_gather.6.part_ref = bf16[4,48,2688]{2,1,0:T(8,128)(2,1)S(1)} all-gather(bf16[1,48,2688]{2,1,0:T(8,128)(2,1)S(1)} %get-tuple-element.29), channel_id=1, replica_groups={{0,32,64,96},{128,160,192,224},{256,288,320,352},{384,416,448,480},{16,..., dimensions={0}, use_global_device_ids=true | all-gather | bytes 1290240 | tf_op jit(solution)/shard_map/all_gather | solution.py:264
  61.7 0.2 shard_map.82
  61.9 13.8 %all_gather.7 = bf16[4,48,2688]{2,1,0:T(8,128)(2,1)S(1)} all-gather(bf16[1,48,2688]{2,1,0:T(8,128)(2,1)S(1)} %shard_map.82), channel_id=1, replica_groups={{0,128,256,384},{32,160,288,416},{64,192,320,448},{96,224,352,480},{16,..., dimensions={0}, use_global_device_ids=true | all-gather | bytes 1290240 | tf_op jit(solution)/shard_map/all_gather | solution.py:266
  75.7 5.8 %collective-permute-start.1 = (bf16[192,2688]{1,0:T(8,128)(2,1)S(1)}, bf16[192,2688]{1,0:T(8,128)(2,1)S(1)}, u32[]{:S(2)}, u32[]{:S(2)}) collective-permute-start(bf16[192,2688]{1,0:T(8,128)(2,1)S(1)} %bitcast.10), channel_id=1, source_target_pairs={{0,16},{16,0},{32,48},{48,32},{64,80},{80,64},{96,112},{112,96},{1... | collective-permute-start | bytes 3096584 | tf_op jit(solution)/shard_map/ppermute | solution.py:268
  81.5 0.6 shard_map.83
  82.1 1.7 %collective-permute-done.1.act_ref = bf16[192,2688]{1,0:T(8,128)(2,1)S(1)} collective-permute-done((bf16[192,2688]{1,0:T(8,128)(2,1)S(1)}, bf16[192,2688]{1,0:T(8,128)(2,1)S(1)}, u32[]{:S(2)}, u32[]{:S(2)}) %collective-permute-start.1) | collective-permute-done | bytes 1032224 | tf_op jit(solution)/shard_map/ppermute | solution.py:268
  83.7 0.6 shard_map.84
  84.3 13.2 %all_to_all.17 = bf16[16,24,256]{2,1,0:T(8,128)(2,1)S(1)} all-to-all(bf16[16,24,256]{2,1,0:T(8,128)(2,1)S(1)} %bitcast.13), channel_id=1, replica_groups=mesh['dp'=32,'expert'=16] {'expert'}, dimensions={0} | all-to-all | bytes 393216 | tf_op jit(solution)/shard_map/all_to_all | solution.py:279
  97.5 0.8 shard_map.85
Async XLA Ops:
  22.7 4.5 %collective-permute-start = (bf16[192,2688]{1,0:T(8,128)(2,1)S(1)}, bf16[192,2688]{1,0:T(8,128)(2,1)S(1)}, u32[]{:S(2)}, u32[]{:S(2)}) collective-permute-start(bf16[192,2688]{1,0:T(8,128)(2,1)S(1)} %get-tuple-element.26), channel_id=1, source_target_pairs={{0,16},{16,0},{32,48},{48,32},{64,80},{80,64},{96,112},{112,96},{1... | collective-permute-start | bytes 3096584 | tf_op jit(solution)/shard_map/ppermute | solution.py:250
  75.7 8.0 %collective-permute-start.1 = (bf16[192,2688]{1,0:T(8,128)(2,1)S(1)}, bf16[192,2688]{1,0:T(8,128)(2,1)S(1)}, u32[]{:S(2)}, u32[]{:S(2)}) collective-permute-start(bf16[192,2688]{1,0:T(8,128)(2,1)S(1)} %bitcast.10), channel_id=1, source_target_pairs={{0,16},{16,0},{32,48},{48,32},{64,80},{80,64},{96,112},{112,96},{1... | collective-permute-start | bytes 3096584 | tf_op jit(solution)/shard_map/ppermute | solution.py:268

commit v5 on v4

--- a/solution.py
+++ b/solution.py
@@ -55,10 +55,10 @@
 
 def call(kernel, out_shape, count, limit_mb=12, flops=0, nbytes=0, **kw):
     kw.setdefault("in_specs", [VMEM] * count)
+    kw.setdefault("out_specs", jax.tree.map(lambda _: VMEM, out_shape))
     return pl.pallas_call(
         kernel,
         out_shape=out_shape,
-        out_specs=jax.tree.map(lambda _: VMEM, out_shape),
         compiler_params=pltpu.CompilerParams(vmem_limit_bytes=limit_mb << 20),
         cost_estimate=pl.CostEstimate(flops=flops, bytes_accessed=nbytes, transcendentals=0),
         **kw,
@@ -73,23 +73,22 @@
     return pl.ds(pl.multiple_of(c * H, H), H), pl.ds(pl.multiple_of(F + c * H, H), H)
 
 
-def fetch_half(wgu_hbm, wd_hbm, wgu_ref, wd_ref, sems, c):
+def fetch_half(wgu_hbm, wd_hbm, refs, sems, c):
     gate, up = half_columns(c)
-    return [
-        pltpu.make_async_copy(wgu_hbm.at[:, gate], wgu_ref.at[:, pl.ds(0, H)], sems.at[0]),
-        pltpu.make_async_copy(wgu_hbm.at[:, up], wgu_ref.at[:, pl.ds(H, H)], sems.at[1]),
-        pltpu.make_async_copy(wd_hbm.at[gate, :], wd_ref, sems.at[2]),
-    ]
+    parts = (wgu_hbm.at[:, gate], wgu_hbm.at[:, up], wd_hbm.at[gate, :])
+    return [pltpu.make_async_copy(p, r, sems.at[n]) for n, (p, r) in enumerate(zip(parts, refs))]
 
 
 def pack_kernel(
     ids_hbm, gate_hbm, tok_hbm, grad_hbm, wgu_hbm, wd_hbm,
-    send_ref, place_ref, weight_ref, wgu_out, wd_out,
-    ids_ref, gate_ref, tok_ref, grad_ref, sems, half_sems,
+    send_hbm, place_ref, weight_ref, *refs,
 ):
+    *weight_refs, ids_ref, gate_ref, tok_ref, grad_ref, send_ref, sems, half_sems = refs
     pairs = [(ids_hbm, ids_ref), (gate_hbm, gate_ref), (tok_hbm, tok_ref), (grad_hbm, grad_ref)]
     moves = [pltpu.make_async_copy(*pair, sems.at[n]) for n, pair in enumerate(pairs)]
-    moves += fetch_half(wgu_hbm, wd_hbm, wgu_out, wd_out, half_sems, 1 - core())
+    moves += fetch_half(wgu_hbm, wd_hbm, weight_refs[:3], half_sems, 1 - core())
+    rows = pl.ds(pl.multiple_of(core() * H, H), H)
+    moves.append(pltpu.make_async_copy(wd_hbm.at[rows, :], weight_refs[3], half_sems.at[3]))
     for move in moves:
         move.start()
     eye = iota((TOK, TOK), 0) == iota((TOK, TOK), 1)
@@ -118,41 +117,47 @@
     pick = onehot((row == first) | (row == second))
     total = mm(pick, jnp.concatenate(values, axis=0))
     send_ref[...] = total.astype(BF16)
+    written = pltpu.make_async_copy(send_ref, send_hbm, sems.at[4])
+    written.start()
     for move in moves[4:]:
         move.wait()
-
-
-def partials(x, g, wgu_ref, wd_ref):
-    return mm(x, wgu_ref[:, :H]), mm(x, wgu_ref[:, H:]), mm_t(g, wd_ref[...])
-
-
-def away_kernel(arr_ref, wgu_ref, wd_ref, out_ref, x_ref, g_ref, pair_ref, sort_ref):
+    written.wait()
+
+
+def partials(rows_ref, gate_ref, up_ref, down_ref):
+    x = rows_ref[:ROWS]
+    return mm(x, gate_ref[...]), mm(x, up_ref[...]), mm_t(rows_ref[ROWS:], down_ref[...])
+
+
+def sort_kernel(arr_ref, rows_ref, pair_ref, sort_ref):
     pair_ref[...] = arr_ref[...].astype(F32)
-    for n, rows_ref in enumerate((x_ref, g_ref)):
+    for n in range(2):
         for b in range(E):
             at = b * PAIR + n * CAP
             sort_ref[b * CAP : (b + 1) * CAP, :] = pair_ref[at : at + CAP, :]
-        rows_ref[...] = sort_ref[...].astype(BF16)
-    terms = partials(x_ref[...], g_ref[...], wgu_ref, wd_ref)
-    for j, term in enumerate(terms):
-        out_ref[:, j * H : (j + 1) * H] = term.astype(BF16)
-
-
-def home_kernel(x_ref, g_ref, wgu_hbm, wd_hbm, out_ref, wgu_out, wd_out, half_sems):
-    moves = fetch_half(wgu_hbm, wd_hbm, wgu_out, wd_out, half_sems, core())
+        rows_ref[n * ROWS : (n + 1) * ROWS] = sort_ref[...].astype(BF16)
+
+
+def home_kernel(rows_ref, down_ref, wgu_hbm, out_ref, gate_ref, up_ref, sems):
+    held = (gate_ref, up_ref)
+    moves = [
+        pltpu.make_async_copy(wgu_hbm.at[:, cols], ref, sems.at[n])
+        for n, (cols, ref) in enumerate(zip(half_columns(core()), held))
+    ]
     for move in moves:
         move.start()
-    for move in moves:
+    out_ref[:, 2 * H :] = mm_t(rows_ref[ROWS:], down_ref[...])
+    for j, (move, w_ref) in enumerate(zip(moves, held)):
         move.wait()
-    terms = partials(x_ref[...], g_ref[...], wgu_out, wd_out)
-    for j, term in enumerate(terms):
-        out_ref[:, j * H : (j + 1) * H] = term
-
-
-def add_kernel(home_ref, got_ref, out_ref, own_ref):
-    out_ref[...] = (home_ref[...] + got_ref[...].astype(F32)).astype(BF16)
-    rows = pl.ds(pl.multiple_of(place_in_first() * RX, RX), RX)
-    own_ref[...] = home_ref[rows, :] + got_ref[rows, :].astype(F32)
+        out_ref[:, j * H : (j + 1) * H] = mm(rows_ref[:ROWS], w_ref[...])
+
+
+def join_kernel(home_ref, rows_ref, gate_ref, up_ref, down_ref, out_ref, own_ref, sum_ref):
+    for j, term in enumerate(partials(rows_ref, gate_ref, up_ref, down_ref)):
+        cols = slice(j * H, (j + 1) * H)
+        sum_ref[:, cols] = home_ref[:, cols] + term
+        out_ref[:, cols] = sum_ref[:, cols].astype(BF16)
+    own_ref[...] = sum_ref[pl.ds(pl.multiple_of(place_in_first() * RX, RX), RX), :]
 
 
 def sum_kernel(got_ref, own_ref, out_ref, rest_ref):
@@ -177,13 +182,19 @@
     out_ref[0, :, 2 * H :] = (hg * silu).astype(BF16)
 
 
-def products(act_ref, wgu_ref, wd_ref):
-    back = mm_t(act_ref[:, H : 2 * H], wgu_ref[:, :H]) + mm_t(act_ref[:, 2 * H :], wgu_ref[:, H:])
-    return mm(act_ref[:, :H], wd_ref[...]), back
-
-
-def first_kernel(act_ref, wgu_ref, wd_ref, place_ref, out_ref, back_ref, pick_ref):
-    out_ref[...], back_ref[...] = products(act_ref, wgu_ref, wd_ref)
+def products(act_ref, gate_ref, up_ref, down_ref):
+    back = mm_t(act_ref[:, H : 2 * H], gate_ref[...]) + mm_t(act_ref[:, 2 * H :], up_ref[...])
+    return mm(act_ref[:, :H], down_ref[...]), back
+
+
+def other_kernel(act_ref, gate_ref, up_ref, down_ref, out_ref):
+    out, back = products(act_ref, gate_ref, up_ref, down_ref)
+    out_ref[:ROWS] = out.astype(BF16)
+    out_ref[ROWS:] = back.astype(BF16)
+
+
+def first_kernel(act_ref, gate_ref, up_ref, down_ref, place_ref, out_ref, pick_ref):
+    out_ref[:ROWS], out_ref[ROWS:] = products(act_ref, gate_ref, up_ref, down_ref)
     col = iota((TOK, SEND), 1)
     at = [place_ref[:, k : k + 1] for k in range(TOPK)]
     for k in range(TOPK):
@@ -191,13 +202,13 @@
     pick_ref[TOPK * TOK :, :] = onehot((col == at[0] + CAP) | (col == at[1] + CAP))
 
 
-def finish_kernel(act_ref, wgu_ref, wd_ref, out_ref, back_ref, send_ref, pair_ref, sort_ref):
-    terms = products(act_ref, wgu_ref, wd_ref)
-    for n, (own_ref, term) in enumerate(zip((out_ref, back_ref), terms)):
-        sort_ref[...] = own_ref[...] + term
+def finish_kernel(own_ref, got_ref, send_ref, pair_ref, sort_ref):
+    sort_ref[...] = own_ref[...] + got_ref[...].astype(F32)
+    for n in range(2):
         for b in range(E):
             at = b * PAIR + n * CAP
-            pair_ref[at : at + CAP, :] = sort_ref[b * CAP : (b + 1) * CAP, :]
+            start = n * ROWS + b * CAP
+            pair_ref[at : at + CAP, :] = sort_ref[start : start + CAP, :]
     send_ref[...] = pair_ref[...].astype(BF16)
 
 
@@ -213,50 +224,48 @@
 def local(tokens, gate_up, down, expert_ids, gate_values, out_grad):
     sds = jax.ShapeDtypeStruct
     wide16, wide32 = (sds((ROWS, 3 * H), t) for t in (BF16, F32))
-    narrow16, narrow32 = (sds((ROWS, DW), t) for t in (BF16, F32))
+    pair16, pair32 = (sds((SEND, DW), t) for t in (BF16, F32))
     chunk16, chunk32 = sds((1, RX, 3 * H), BF16), sds((RX, 3 * H), F32)
+    half = (sds((DW, H), BF16), sds((DW, H), BF16), sds((H, DW), BF16))
     small = [pltpu.VMEM((TOPK, TOK), jnp.int32), pltpu.VMEM((TOPK, TOK), F32)]
-    small += [pltpu.VMEM((TOK, DW), BF16)] * 2
-    half = (sds((DW, 2 * H), BF16), sds((H, DW), BF16))
+    small += [pltpu.VMEM((TOK, DW), BF16)] * 2 + [pltpu.VMEM((SEND, DW), BF16)]
+    sort = [pltpu.VMEM((SEND, DW), F32), pltpu.VMEM((ROWS, DW), F32)]
     hbm = pl.BlockSpec(memory_space=pltpu.HBM)
     in_hbm = lambda *vs: [pltpu.with_memory_space_constraint(v, pltpu.HBM) for v in vs]
     wgu, wd = in_hbm(gate_up[0], down[0])
     work = dict(flops=2 * ROWS * DW * 3 * H, nbytes=4 << 20)
 
-    send, place, weight, wgu_away, wd_away = call(
+    send, place, weight, *theirs, held_down = call(
         pack_kernel,
-        (
-            sds((SEND, DW), BF16),
-            sds((TOK, TOPK), jnp.int32),
-            sds((TOK, TOPK), F32),
-            *half,
-        ),
+        (pair16, sds((TOK, TOPK), jnp.int32), sds((TOK, TOPK), F32), *half, half[2]),
         6,
         in_specs=[hbm] * 6,
-        scratch_shapes=small + [pltpu.SemaphoreType.DMA((n,)) for n in (4, 3)],
+        out_specs=(hbm, *[VMEM] * 6),
+        scratch_shapes=small + [pltpu.SemaphoreType.DMA((n,)) for n in (5, 4)],
     )(*in_hbm(expert_ids.T, gate_values.T, tokens, out_grad), wgu, wd)
+    cross = [lax.ppermute(w, "dp", SWAP) for w in theirs]
     arrived = lax.all_to_all(
         send.reshape(E, PAIR, DW), "expert", 0, 0, tiled=True
     ).reshape(SEND, DW)
-    away, x, g = call(
-        away_kernel,
-        (wide16, narrow16, narrow16),
+    rows = call(sort_kernel, pair16, 1, scratch_shapes=sort)(arrived)
+    other = lax.ppermute(rows, "dp", SWAP)
+    home, *held = call(
+        home_kernel,
+        (wide32, *half[:2]),
         3,
-        scratch_shapes=[pltpu.VMEM((SEND, DW), F32), pltpu.VMEM((ROWS, DW), F32)],
+        in_specs=[VMEM, VMEM, hbm],
+        scratch_shapes=[pltpu.SemaphoreType.DMA((2,))],
         **work,
-    )(
-        arrived, wgu_away, wd_away
-    )
-    got = lax.ppermute(away, "dp", SWAP)
-    home, wgu_home, wd_home = call(
-        home_kernel,
-        (wide32, *half),
-        4,
-        in_specs=[VMEM, VMEM, hbm, hbm],
-        scratch_shapes=[pltpu.SemaphoreType.DMA((3,))],
+    )(rows, held_down, wgu)
+    held.append(held_down)
+    chip, own = call(
+        join_kernel,
+        (wide16, chunk32),
+        5,
+        limit_mb=16,
+        scratch_shapes=[pltpu.VMEM((ROWS, 3 * H), F32)],
         **work,
-    )(x, g, wgu, wd)
-    chip, own = call(add_kernel, (wide16, chunk32), 2)(home, got)
+    )(home, other, *cross)
     got = lax.all_to_all(
         chip.reshape(RING, RX, 3 * H), "dp", 0, 0, axis_index_groups=FIRST, tiled=True
     )
@@ -265,17 +274,12 @@
     act = call(act_kernel, chunk16, 2)(parts, rest)
     mine = lax.all_gather(act, "dp", axis=0, axis_index_groups=FIRST, tiled=True)
     mine = mine.reshape(ROWS, 3 * H)
-    other = lax.ppermute(mine, "dp", SWAP)
+    terms = call(other_kernel, pair16, 4, **work)(mine, *cross)
+    got = lax.ppermute(terms, "dp", SWAP)
     pick = sds(((TOPK + 1) * TOK, SEND), BF16)
-    out, back, pick = call(first_kernel, (narrow32, narrow32, pick), 4, **work)(
-        mine, wgu_home, wd_home, place
-    )
-    back = call(
-        finish_kernel,
-        sds((SEND, DW), BF16),
-        5,
-        scratch_shapes=[pltpu.VMEM((SEND, DW), F32), pltpu.VMEM((ROWS, DW), F32)],
-    )(other, wgu_away, wd_away, out, back)
+    terms, pick = call(first_kernel, (pair32, pick), 5, **work)(mine, *held, place)
+    sort[1] = pltpu.VMEM((SEND, DW), F32)
+    back = call(finish_kernel, pair16, 2, scratch_shapes=sort)(terms, got)
     returned = lax.all_to_all(
         back.reshape(E, PAIR, DW), "expert", 0, 0, tiled=True
     ).reshape(SEND, DW)

time: 98.7 us -> 98.6 us (level)
  blocking collectives: 81 us -> 63 us
  starting transfers between devices: 7.67 us -> 24.8 us
    all_to_all x1 -> x0, blocking collectives: 20.1 us -> none  [local(): lax.all_to_all(send.reshape(E, PAIR, DW), 'expert', 0, 0, tiled=True)]
    all_to_all x0 -> x1, starting transfers between devices: none -> 11.8 us  [local(): lax.all_to_all(send.reshape(E, PAIR, DW), 'expert', 0, 0, tiled=True)]
    ppermute x2 -> x5, starting transfers between devices: 7.67 us -> 13 us  [the longest x3 6.24 us: local(): cross = [lax.ppermute(w, 'dp', SWAP) for w in theirs]]
    all_to_all x0 -> x1, waiting for transfers between devices: none -> 2.23 us  [local(): lax.all_to_all(send.reshape(E, PAIR, DW), 'expert', 0, 0, tiled=True)]
    ppermute x2 -> x5, waiting for transfers between devices: 2.39 us -> 0.48 us  [the longest x1 0.47 us: local(): got = lax.ppermute(terms, 'dp', SWAP)]
    all_to_all x1, blocking collectives: 13.2 us -> 14.3 us  [local(): lax.all_to_all(back.reshape(E, PAIR, DW), 'expert', 0, 0, tiled=True)]
    pallas_call x6 -> x7, Pallas kernels: 5.3 us -> 5.56 us  [the longest x1 1.99 us: local(): call(pack_kernel, (pair16, sds((TOK, TOPK), jnp.int32), sds((TOK, TOPK),...]
  transfers between devices with their start and end apart: 2 -> 6, of which waited for: 2 -> 2; matrix products, arithmetic and copies ran while one was open for 0% -> 0% of each run, Pallas kernels for 2% -> 2%
where the time goes in v5:
time: 98.6 us; the launch traced here: 98.1 us
  blocking collectives  63 us (64%)
  starting transfers between devices  24.8 us (25%)
  Pallas kernels  6.87 us (7%)
  waiting for transfers between devices  2.71 us (3%)
    all_gather x1, blocking collectives, local(): lax.all_gather(chunk, 'dp', axis=0, axis_index_groups=SECOND, tiled=True)  20 us
    all_to_all x1, blocking collectives, local(): lax.all_to_all(chip.reshape(RING, RX, 3 * H), 'dp', 0, 0, axis_index_grou...  14.9 us
    all_to_all x1, blocking collectives, local(): lax.all_to_all(back.reshape(E, PAIR, DW), 'expert', 0, 0, tiled=True)  14.3 us
    all_gather x1, blocking collectives, local(): lax.all_gather(act, 'dp', axis=0, axis_index_groups=FIRST, tiled=True)  13.8 us
    all_to_all x1, starting transfers between devices, local(): lax.all_to_all(send.reshape(E, PAIR, DW), 'expert', 0, 0, tiled=True)  11.8 us
    ppermute x3, starting transfers between devices, local(): cross = [lax.ppermute(w, 'dp', SWAP) for w in theirs]  6.24 us
    ppermute x1, starting transfers between devices, local(): got = lax.ppermute(terms, 'dp', SWAP)  4.81 us
    all_to_all x1, waiting for transfers between devices, local(): lax.all_to_all(send.reshape(E, PAIR, DW), 'expert', 0, 0, tiled=True)  2.23 us
  transfers between devices with their start and end apart: 6, of which 2 were waited for; matrix products, arithmetic and copies ran while one was open for 0% of the time, Pallas kernels for 2%

profile of v5, /device:TPU:8, one launch (start us, length us, event | category | flops | bytes accessed | tf_op | source)
XLA Modules:
  0.0 98.1 jit_solution(500673971177335753)
XLA Ops:
  0.6 2.0 %shard_map.77 = (bf16[384,256]{1,0:T(8,128)(2,1)}, s32[64,2]{1,0:T(8,128)S(1)}, f32[64,2]{1,0:T(8,128)S(1)}, bf16[256,896]{1,0:T(8,128)(2,1)S(1)}, bf16[256,896]...) custom-call(s32[2,64]{1,0:T(2,128)} %bitcast.19, f32[2,64]{1,0:T(2,128)} %bitcast.20, ...), custom_call_target="tpu_custom_call" | custom-call | tf_op jit(solution)/shard_map/pallas_call | solution.py:238
  2.6 11.8 %all-to-all-start = ((bf16[16,24,256]{2,1,0:T(8,128)(2,1)}), bf16[16,24,256]{2,1,0:T(8,128)(2,1)S(1)}, u32[]{:S(2)}, u32[]{:S(2)}) async-start(bf16[16,24,256]{2,1,0:T(8,128)(2,1)} %bitcast.4), calls=%async_computation | async-start | bytes 393216 | tf_op jit(solution)/shard_map/all_to_all | solution.py:247
  14.4 1.9 %collective-permute-start.1 = (bf16[256,896]{1,0:T(8,128)(2,1)S(1)}, bf16[256,896]{1,0:T(8,128)(2,1)S(1)}, u32[]{:S(2)}, u32[]{:S(2)}) collective-permute-start(bf16[256,896]{1,0:T(8,128)(2,1)S(1)} %get-tuple-element.21), channel_id=1, source_target_pairs={{0,16},{16,0},{32,48},{48,32},{64,80},{80,64},{96,112},{112,96},{1... | collective-permute-start | bytes 1376264 | tf_op jit(solution)/shard_map/ppermute | solution.py:246
  16.3 2.4 %collective-permute-start.2 = (bf16[256,896]{1,0:T(8,128)(2,1)S(1)}, bf16[256,896]{1,0:T(8,128)(2,1)S(1)}, u32[]{:S(2)}, u32[]{:S(2)}) collective-permute-start(bf16[256,896]{1,0:T(8,128)(2,1)S(1)} %get-tuple-element.22), channel_id=1, source_target_pairs={{0,16},{16,0},{32,48},{48,32},{64,80},{80,64},{96,112},{112,96},{1... | collective-permute-start | bytes 1376264 | tf_op jit(solution)/shard_map/ppermute | solution.py:246
  18.8 1.9 %collective-permute-start.3 = (bf16[896,256]{1,0:T(8,128)(2,1)S(1)}, bf16[896,256]{1,0:T(8,128)(2,1)S(1)}, u32[]{:S(2)}, u32[]{:S(2)}) collective-permute-start(bf16[896,256]{1,0:T(8,128)(2,1)S(1)} %get-tuple-element.23), channel_id=1, source_target_pairs={{0,16},{16,0},{32,48},{48,32},{64,80},{80,64},{96,112},{112,96},{1... | collective-permute-start | bytes 1376264 | tf_op jit(solution)/shard_map/ppermute | solution.py:246
  20.7 2.2 %all-to-all-done = bf16[16,24,256]{2,1,0:T(8,128)(2,1)S(1)} async-done(((bf16[16,24,256]{2,1,0:T(8,128)(2,1)}), bf16[16,24,256]{2,1,0:T(8,128)(2,1)S(1)}, u32[]{:S(2)}, u32[]{:S(2)}) %all-to-all-start) | async-done | bytes 196640 | tf_op jit(solution)/shard_map/all_to_all | solution.py:247
  22.9 0.1 shard_map.78.rows_ref
  23.0 1.9 %collective-permute-start = (bf16[384,256]{1,0:T(8,128)(2,1)S(1)}, bf16[384,256]{1,0:T(8,128)(2,1)S(1)}, u32[]{:S(2)}, u32[]{:S(2)}) collective-permute-start(bf16[384,256]{1,0:T(8,128)(2,1)S(1)} %shard_map.78.rows_ref), channel_id=1, source_target_pairs={{0,16},{16,0},{32,48},{48,32},{64,80},{80,64},{96,112},{112,96},{1... | collective-permute-start | bytes 589832 | tf_op jit(solution)/shard_map/ppermute | solution.py:251
  24.9 1.7 %shard_map.79 = (f32[192,2688]{1,0:T(8,128)S(1)}, bf16[256,896]{1,0:T(8,128)(2,1)S(1)}, bf16[256,896]{1,0:T(8,128)(2,1)S(1)}) custom-call(bf16[384,256]{1,0:T(8,128)(2,1)S(1)} %shard_map.78.rows_ref, bf16[896,256]{1,0:T(8,128)(2,1)S(1)} %get-tuple-element.19.down_ref, bf16[256,3584]{1,0:T(8,128)(2,1)} %bitcast.17), custom_call_target="tpu_custom_call" | custom-call | flops 264241152 | bytes 4194304 | tf_op jit(solution)/shard_map/pallas_call | solution.py:252
  26.6 0.0 collective-permute-done.1.gate_ref
  26.7 0.0 collective-permute-done.rows_ref
  26.7 0.6 shard_map.80
  27.3 14.9 %all_to_all.15.got_ref = bf16[4,48,2688]{2,1,0:T(8,128)(2,1)S(1)} all-to-all(bf16[4,48,2688]{2,1,0:T(8,128)(2,1)S(1)} %bitcast.12), channel_id=1, replica_groups={{0,128,256,384},{32,160,288,416},{64,192,320,448},{96,224,352,480},{16,..., dimensions={0} | all-to-all | bytes 2064384 | tf_op jit(solution)/shard_map/all_to_all | solution.py:269
  42.2 0.3 shard_map.81
  42.4 20.0 %all_gather.6.part_ref = bf16[4,48,2688]{2,1,0:T(8,128)(2,1)S(1)} all-gather(bf16[1,48,2688]{2,1,0:T(8,128)(2,1)S(1)} %get-tuple-element.26), channel_id=1, replica_groups={{0,32,64,96},{128,160,192,224},{256,288,320,352},{384,416,448,480},{16,..., dimensions={0}, use_global_device_ids=true | all-gather | bytes 1290240 | tf_op jit(solution)/shard_map/all_gather | solution.py:273
  62.4 0.2 shard_map.82
  62.7 13.8 %all_gather.7 = bf16[4,48,2688]{2,1,0:T(8,128)(2,1)S(1)} all-gather(bf16[1,48,2688]{2,1,0:T(8,128)(2,1)S(1)} %shard_map.82), channel_id=1, replica_groups={{0,128,256,384},{32,160,288,416},{64,192,320,448},{96,224,352,480},{16,..., dimensions={0}, use_global_device_ids=true | all-gather | bytes 1290240 | tf_op jit(solution)/shard_map/all_gather | solution.py:275
  76.5 0.6 shard_map.84
  77.0 4.8 %collective-permute-start.4 = (bf16[384,256]{1,0:T(8,128)(2,1)S(1)}, bf16[384,256]{1,0:T(8,128)(2,1)S(1)}, u32[]{:S(2)}, u32[]{:S(2)}) collective-permute-start(bf16[384,256]{1,0:T(8,128)(2,1)S(1)} %shard_map.84), channel_id=1, source_target_pairs={{0,16},{16,0},{32,48},{48,32},{64,80},{80,64},{96,112},{112,96},{1... | collective-permute-start | bytes 589832 | tf_op jit(solution)/shard_map/ppermute | solution.py:278
  81.9 0.6 shard_map.83
  82.4 0.5 collective-permute-done.4.got_ref
  82.9 0.1 shard_map.85
  83.0 14.3 %all_to_all.16 = bf16[16,24,256]{2,1,0:T(8,128)(2,1)S(1)} all-to-all(bf16[16,24,256]{2,1,0:T(8,128)(2,1)S(1)} %bitcast.15), channel_id=1, replica_groups=mesh['dp'=32,'expert'=16] {'expert'}, dimensions={0} | all-to-all | bytes 393216 | tf_op jit(solution)/shard_map/all_to_all | solution.py:283
  97.3 0.8 shard_map.86
  (2 shorter events, 0.0 us)
Async XLA Ops:
  2.6 20.3 %all-to-all-start = ((bf16[16,24,256]{2,1,0:T(8,128)(2,1)}), bf16[16,24,256]{2,1,0:T(8,128)(2,1)S(1)}, u32[]{:S(2)}, u32[]{:S(2)}) async-start(bf16[16,24,256]{2,1,0:T(8,128)(2,1)} %bitcast.4), calls=%async_computation | async-start | bytes 393216 | tf_op jit(solution)/shard_map/all_to_all | solution.py:247
  14.4 12.2 %collective-permute-start.1 = (bf16[256,896]{1,0:T(8,128)(2,1)S(1)}, bf16[256,896]{1,0:T(8,128)(2,1)S(1)}, u32[]{:S(2)}, u32[]{:S(2)}) collective-permute-start(bf16[256,896]{1,0:T(8,128)(2,1)S(1)} %get-tuple-element.21), channel_id=1, source_target_pairs={{0,16},{16,0},{32,48},{48,32},{64,80},{80,64},{96,112},{112,96},{1... | collective-permute-start | bytes 1376264 | tf_op jit(solution)/shard_map/ppermute | solution.py:246
  16.3 10.3 %collective-permute-start.2 = (bf16[256,896]{1,0:T(8,128)(2,1)S(1)}, bf16[256,896]{1,0:T(8,128)(2,1)S(1)}, u32[]{:S(2)}, u32[]{:S(2)}) collective-permute-start(bf16[256,896]{1,0:T(8,128)(2,1)S(1)} %get-tuple-element.22), channel_id=1, source_target_pairs={{0,16},{16,0},{32,48},{48,32},{64,80},{80,64},{96,112},{112,96},{1... | collective-permute-start | bytes 1376264 | tf_op jit(solution)/shard_map/ppermute | solution.py:246
  18.8 7.9 %collective-permute-start.3 = (bf16[896,256]{1,0:T(8,128)(2,1)S(1)}, bf16[896,256]{1,0:T(8,128)(2,1)S(1)}, u32[]{:S(2)}, u32[]{:S(2)}) collective-permute-start(bf16[896,256]{1,0:T(8,128)(2,1)S(1)} %get-tuple-element.23), channel_id=1, source_target_pairs={{0,16},{16,0},{32,48},{48,32},{64,80},{80,64},{96,112},{112,96},{1... | collective-permute-start | bytes 1376264 | tf_op jit(solution)/shard_map/ppermute | solution.py:246
  23.0 3.7 %collective-permute-start = (bf16[384,256]{1,0:T(8,128)(2,1)S(1)}, bf16[384,256]{1,0:T(8,128)(2,1)S(1)}, u32[]{:S(2)}, u32[]{:S(2)}) collective-permute-start(bf16[384,256]{1,0:T(8,128)(2,1)S(1)} %shard_map.78.rows_ref), channel_id=1, source_target_pairs={{0,16},{16,0},{32,48},{48,32},{64,80},{80,64},{96,112},{112,96},{1... | collective-permute-start | bytes 589832 | tf_op jit(solution)/shard_map/ppermute | solution.py:251
  77.0 5.9 %collective-permute-start.4 = (bf16[384,256]{1,0:T(8,128)(2,1)S(1)}, bf16[384,256]{1,0:T(8,128)(2,1)S(1)}, u32[]{:S(2)}, u32[]{:S(2)}) collective-permute-start(bf16[384,256]{1,0:T(8,128)(2,1)S(1)} %shard_map.84), channel_id=1, source_target_pairs={{0,16},{16,0},{32,48},{48,32},{64,80},{80,64},{96,112},{112,96},{1... | collective-permute-start | bytes 589832 | tf_op jit(solution)/shard_map/ppermute | solution.py:278

commit v6 on v5

--- a/solution.py
+++ b/solution.py
@@ -98,14 +98,12 @@
     ids = ids_ref[...]
     hots = [(ids[k : k + 1, :] == iota((E, TOK), 0)).astype(F32) for k in range(TOPK)]
     earlier = mm((hots[0] + hots[1]).astype(BF16), before)
-    across, places, weights = [], [], []
+    across, weights = [], []
     for k in range(TOPK):
         rank = jnp.sum(hots[k] * earlier, axis=0, keepdims=True).astype(jnp.int32)
         place = ids[k : k + 1, :] * PAIR + rank
         across.append(place)
-        places.append(turned(place, eye))
         weights.append(turned(gate_ref[k : k + 1, :], eye))
-    place_ref[...] = jnp.concatenate(places, axis=1)
     weight_ref[...] = jnp.concatenate(weights, axis=1)
     moves[2].wait()
     moves[3].wait()
@@ -115,13 +113,20 @@
     second = jnp.concatenate(across[1:2] + [at + CAP for at in across], axis=1)
     row = iota((SEND, TOK * (TOPK + 1)), 0)
     pick = onehot((row == first) | (row == second))
-    total = mm(pick, jnp.concatenate(values, axis=0))
-    send_ref[...] = total.astype(BF16)
-    written = pltpu.make_async_copy(send_ref, send_hbm, sems.at[4])
-    written.start()
+    values = jnp.concatenate(values, axis=0)
+    written = []
+    for n in range(2):
+        rows = pl.ds(n * (SEND // 2), SEND // 2)
+        send_ref[rows, :] = mm(pick[n * (SEND // 2) : (n + 1) * (SEND // 2)], values).astype(BF16)
+        written.append(
+            pltpu.make_async_copy(send_ref.at[rows, :], send_hbm.at[rows, :], sems.at[4 + n])
+        )
+        written[n].start()
+    place_ref[...] = jnp.concatenate([turned(place, eye) for place in across], axis=1)
     for move in moves[4:]:
         move.wait()
-    written.wait()
+    for move in written:
+        move.wait()
 
 
 def partials(rows_ref, gate_ref, up_ref, down_ref):
@@ -241,7 +246,7 @@
         6,
         in_specs=[hbm] * 6,
         out_specs=(hbm, *[VMEM] * 6),
-        scratch_shapes=small + [pltpu.SemaphoreType.DMA((n,)) for n in (5, 4)],
+        scratch_shapes=small + [pltpu.SemaphoreType.DMA((n,)) for n in (6, 4)],
     )(*in_hbm(expert_ids.T, gate_values.T, tokens, out_grad), wgu, wd)
     cross = [lax.ppermute(w, "dp", SWAP) for w in theirs]
     arrived = lax.all_to_all(

time: 98.6 us -> 98.4 us (level)
  no operation moved by 1% of the time
where the time goes in v6:
time: 98.4 us; the launch traced here: 98 us
  blocking collectives  63 us (64%)
  starting transfers between devices  24.8 us (25%)
  Pallas kernels  6.75 us (7%)
  waiting for transfers between devices  2.7 us (3%)
    all_gather x1, blocking collectives, local(): lax.all_gather(chunk, 'dp', axis=0, axis_index_groups=SECOND, tiled=True)  20 us
    all_to_all x1, blocking collectives, local(): lax.all_to_all(chip.reshape(RING, RX, 3 * H), 'dp', 0, 0, axis_index_grou...  14.9 us
    all_to_all x1, blocking collectives, local(): lax.all_to_all(back.reshape(E, PAIR, DW), 'expert', 0, 0, tiled=True)  14.3 us
    all_gather x1, blocking collectives, local(): lax.all_gather(act, 'dp', axis=0, axis_index_groups=FIRST, tiled=True)  13.8 us
    all_to_all x1, starting transfers between devices, local(): lax.all_to_all(send.reshape(E, PAIR, DW), 'expert', 0, 0, tiled=True)  11.8 us
    ppermute x3, starting transfers between devices, local(): cross = [lax.ppermute(w, 'dp', SWAP) for w in theirs]  6.24 us
    ppermute x1, starting transfers between devices, local(): got = lax.ppermute(terms, 'dp', SWAP)  4.82 us
    all_to_all x1, waiting for transfers between devices, local(): lax.all_to_all(send.reshape(E, PAIR, DW), 'expert', 0, 0, tiled=True)  2.23 us
  transfers between devices with their start and end apart: 6, of which 2 were waited for; matrix products, arithmetic and copies ran while one was open for 0% of the time, Pallas kernels for 2%

profile of v6, /device:TPU:8, one launch (start us, length us, event | category | flops | bytes accessed | tf_op | source)
XLA Modules:
  0.0 98.0 jit_solution(3726930321883731721)
XLA Ops:
  0.6 1.9 %shard_map.77 = (bf16[384,256]{1,0:T(8,128)(2,1)}, s32[64,2]{1,0:T(8,128)S(1)}, f32[64,2]{1,0:T(8,128)S(1)}, bf16[256,896]{1,0:T(8,128)(2,1)S(1)}, bf16[256,896]...) custom-call(s32[2,64]{1,0:T(2,128)} %bitcast.19, f32[2,64]{1,0:T(2,128)} %bitcast.20, ...), custom_call_target="tpu_custom_call" | custom-call | tf_op jit(solution)/shard_map/pallas_call | solution.py:243
  2.5 11.8 %all-to-all-start = ((bf16[16,24,256]{2,1,0:T(8,128)(2,1)}), bf16[16,24,256]{2,1,0:T(8,128)(2,1)S(1)}, u32[]{:S(2)}, u32[]{:S(2)}) async-start(bf16[16,24,256]{2,1,0:T(8,128)(2,1)} %bitcast.4), calls=%async_computation | async-start | bytes 393216 | tf_op jit(solution)/shard_map/all_to_all | solution.py:252
  14.3 1.9 %collective-permute-start.1 = (bf16[256,896]{1,0:T(8,128)(2,1)S(1)}, bf16[256,896]{1,0:T(8,128)(2,1)S(1)}, u32[]{:S(2)}, u32[]{:S(2)}) collective-permute-start(bf16[256,896]{1,0:T(8,128)(2,1)S(1)} %get-tuple-element.21), channel_id=1, source_target_pairs={{0,16},{16,0},{32,48},{48,32},{64,80},{80,64},{96,112},{112,96},{1... | collective-permute-start | bytes 1376264 | tf_op jit(solution)/shard_map/ppermute | solution.py:251
  16.2 2.4 %collective-permute-start.2 = (bf16[256,896]{1,0:T(8,128)(2,1)S(1)}, bf16[256,896]{1,0:T(8,128)(2,1)S(1)}, u32[]{:S(2)}, u32[]{:S(2)}) collective-permute-start(bf16[256,896]{1,0:T(8,128)(2,1)S(1)} %get-tuple-element.22), channel_id=1, source_target_pairs={{0,16},{16,0},{32,48},{48,32},{64,80},{80,64},{96,112},{112,96},{1... | collective-permute-start | bytes 1376264 | tf_op jit(solution)/shard_map/ppermute | solution.py:251
  18.7 1.9 %collective-permute-start.3 = (bf16[896,256]{1,0:T(8,128)(2,1)S(1)}, bf16[896,256]{1,0:T(8,128)(2,1)S(1)}, u32[]{:S(2)}, u32[]{:S(2)}) collective-permute-start(bf16[896,256]{1,0:T(8,128)(2,1)S(1)} %get-tuple-element.23), channel_id=1, source_target_pairs={{0,16},{16,0},{32,48},{48,32},{64,80},{80,64},{96,112},{112,96},{1... | collective-permute-start | bytes 1376264 | tf_op jit(solution)/shard_map/ppermute | solution.py:251
  20.6 2.2 %all-to-all-done = bf16[16,24,256]{2,1,0:T(8,128)(2,1)S(1)} async-done(((bf16[16,24,256]{2,1,0:T(8,128)(2,1)}), bf16[16,24,256]{2,1,0:T(8,128)(2,1)S(1)}, u32[]{:S(2)}, u32[]{:S(2)}) %all-to-all-start) | async-done | bytes 196640 | tf_op jit(solution)/shard_map/all_to_all | solution.py:252
  22.8 0.1 shard_map.78.rows_ref
  22.9 1.9 %collective-permute-start = (bf16[384,256]{1,0:T(8,128)(2,1)S(1)}, bf16[384,256]{1,0:T(8,128)(2,1)S(1)}, u32[]{:S(2)}, u32[]{:S(2)}) collective-permute-start(bf16[384,256]{1,0:T(8,128)(2,1)S(1)} %shard_map.78.rows_ref), channel_id=1, source_target_pairs={{0,16},{16,0},{32,48},{48,32},{64,80},{80,64},{96,112},{112,96},{1... | collective-permute-start | bytes 589832 | tf_op jit(solution)/shard_map/ppermute | solution.py:256
  24.8 1.7 %shard_map.79 = (f32[192,2688]{1,0:T(8,128)S(1)}, bf16[256,896]{1,0:T(8,128)(2,1)S(1)}, bf16[256,896]{1,0:T(8,128)(2,1)S(1)}) custom-call(bf16[384,256]{1,0:T(8,128)(2,1)S(1)} %shard_map.78.rows_ref, bf16[896,256]{1,0:T(8,128)(2,1)S(1)} %get-tuple-element.19.down_ref, bf16[256,3584]{1,0:T(8,128)(2,1)} %bitcast.17), custom_call_target="tpu_custom_call" | custom-call | flops 264241152 | bytes 4194304 | tf_op jit(solution)/shard_map/pallas_call | solution.py:257
  26.5 0.0 collective-permute-done.1.gate_ref
  26.5 0.0 collective-permute-done.3.down_ref
  26.6 0.6 shard_map.80
  27.1 14.9 %all_to_all.15.got_ref = bf16[4,48,2688]{2,1,0:T(8,128)(2,1)S(1)} all-to-all(bf16[4,48,2688]{2,1,0:T(8,128)(2,1)S(1)} %bitcast.12), channel_id=1, replica_groups={{0,128,256,384},{32,160,288,416},{64,192,320,448},{96,224,352,480},{16,..., dimensions={0} | all-to-all | bytes 2064384 | tf_op jit(solution)/shard_map/all_to_all | solution.py:274
  42.1 0.3 shard_map.81
  42.3 20.0 %all_gather.6.part_ref = bf16[4,48,2688]{2,1,0:T(8,128)(2,1)S(1)} all-gather(bf16[1,48,2688]{2,1,0:T(8,128)(2,1)S(1)} %get-tuple-element.26), channel_id=1, replica_groups={{0,32,64,96},{128,160,192,224},{256,288,320,352},{384,416,448,480},{16,..., dimensions={0}, use_global_device_ids=true | all-gather | bytes 1290240 | tf_op jit(solution)/shard_map/all_gather | solution.py:278
  62.3 0.2 shard_map.82
  62.6 13.8 %all_gather.7 = bf16[4,48,2688]{2,1,0:T(8,128)(2,1)S(1)} all-gather(bf16[1,48,2688]{2,1,0:T(8,128)(2,1)S(1)} %shard_map.82), channel_id=1, replica_groups={{0,128,256,384},{32,160,288,416},{64,192,320,448},{96,224,352,480},{16,..., dimensions={0}, use_global_device_ids=true | all-gather | bytes 1290240 | tf_op jit(solution)/shard_map/all_gather | solution.py:280
  76.4 0.6 shard_map.84
  76.9 4.8 %collective-permute-start.4 = (bf16[384,256]{1,0:T(8,128)(2,1)S(1)}, bf16[384,256]{1,0:T(8,128)(2,1)S(1)}, u32[]{:S(2)}, u32[]{:S(2)}) collective-permute-start(bf16[384,256]{1,0:T(8,128)(2,1)S(1)} %shard_map.84), channel_id=1, source_target_pairs={{0,16},{16,0},{32,48},{48,32},{64,80},{80,64},{96,112},{112,96},{1... | collective-permute-start | bytes 589832 | tf_op jit(solution)/shard_map/ppermute | solution.py:283
  81.8 0.6 shard_map.83
  82.3 0.5 collective-permute-done.4.got_ref
  82.8 0.1 shard_map.85
  82.9 14.3 %all_to_all.16 = bf16[16,24,256]{2,1,0:T(8,128)(2,1)S(1)} all-to-all(bf16[16,24,256]{2,1,0:T(8,128)(2,1)S(1)} %bitcast.15), channel_id=1, replica_groups=mesh['dp'=32,'expert'=16] {'expert'}, dimensions={0} | all-to-all | bytes 393216 | tf_op jit(solution)/shard_map/all_to_all | solution.py:288
  97.2 0.8 shard_map.86
  (2 shorter events, 0.0 us)
Async XLA Ops:
  2.5 20.3 %all-to-all-start = ((bf16[16,24,256]{2,1,0:T(8,128)(2,1)}), bf16[16,24,256]{2,1,0:T(8,128)(2,1)S(1)}, u32[]{:S(2)}, u32[]{:S(2)}) async-start(bf16[16,24,256]{2,1,0:T(8,128)(2,1)} %bitcast.4), calls=%async_computation | async-start | bytes 393216 | tf_op jit(solution)/shard_map/all_to_all | solution.py:252
  14.3 12.2 %collective-permute-start.1 = (bf16[256,896]{1,0:T(8,128)(2,1)S(1)}, bf16[256,896]{1,0:T(8,128)(2,1)S(1)}, u32[]{:S(2)}, u32[]{:S(2)}) collective-permute-start(bf16[256,896]{1,0:T(8,128)(2,1)S(1)} %get-tuple-element.21), channel_id=1, source_target_pairs={{0,16},{16,0},{32,48},{48,32},{64,80},{80,64},{96,112},{112,96},{1... | collective-permute-start | bytes 1376264 | tf_op jit(solution)/shard_map/ppermute | solution.py:251
  16.2 10.3 %collective-permute-start.2 = (bf16[256,896]{1,0:T(8,128)(2,1)S(1)}, bf16[256,896]{1,0:T(8,128)(2,1)S(1)}, u32[]{:S(2)}, u32[]{:S(2)}) collective-permute-start(bf16[256,896]{1,0:T(8,128)(2,1)S(1)} %get-tuple-element.22), channel_id=1, source_target_pairs={{0,16},{16,0},{32,48},{48,32},{64,80},{80,64},{96,112},{112,96},{1... | collective-permute-start | bytes 1376264 | tf_op jit(solution)/shard_map/ppermute | solution.py:251
  18.7 7.9 %collective-permute-start.3 = (bf16[896,256]{1,0:T(8,128)(2,1)S(1)}, bf16[896,256]{1,0:T(8,128)(2,1)S(1)}, u32[]{:S(2)}, u32[]{:S(2)}) collective-permute-start(bf16[896,256]{1,0:T(8,128)(2,1)S(1)} %get-tuple-element.23), channel_id=1, source_target_pairs={{0,16},{16,0},{32,48},{48,32},{64,80},{80,64},{96,112},{112,96},{1... | collective-permute-start | bytes 1376264 | tf_op jit(solution)/shard_map/ppermute | solution.py:251
  22.9 3.7 %collective-permute-start = (bf16[384,256]{1,0:T(8,128)(2,1)S(1)}, bf16[384,256]{1,0:T(8,128)(2,1)S(1)}, u32[]{:S(2)}, u32[]{:S(2)}) collective-permute-start(bf16[384,256]{1,0:T(8,128)(2,1)S(1)} %shard_map.78.rows_ref), channel_id=1, source_target_pairs={{0,16},{16,0},{32,48},{48,32},{64,80},{80,64},{96,112},{112,96},{1... | collective-permute-start | bytes 589832 | tf_op jit(solution)/shard_map/ppermute | solution.py:256
  76.9 5.9 %collective-permute-start.4 = (bf16[384,256]{1,0:T(8,128)(2,1)S(1)}, bf16[384,256]{1,0:T(8,128)(2,1)S(1)}, u32[]{:S(2)}, u32[]{:S(2)}) collective-permute-start(bf16[384,256]{1,0:T(8,128)(2,1)S(1)} %shard_map.84), channel_id=1, source_target_pairs={{0,16},{16,0},{32,48},{48,32},{64,80},{80,64},{96,112},{112,96},{1... | collective-permute-start | bytes 589832 | tf_op jit(solution)/shard_map/ppermute | solution.py:283

commit v7 on v6

--- a/solution.py
+++ b/solution.py
@@ -157,27 +157,22 @@
         out_ref[:, j * H : (j + 1) * H] = mm(rows_ref[:ROWS], w_ref[...])
 
 
-def join_kernel(home_ref, rows_ref, gate_ref, up_ref, down_ref, out_ref, own_ref, sum_ref):
+def join_kernel(home_ref, rows_ref, gate_ref, up_ref, down_ref, out_ref):
     for j, term in enumerate(partials(rows_ref, gate_ref, up_ref, down_ref)):
         cols = slice(j * H, (j + 1) * H)
-        sum_ref[:, cols] = home_ref[:, cols] + term
-        out_ref[:, cols] = sum_ref[:, cols].astype(BF16)
-    own_ref[...] = sum_ref[pl.ds(pl.multiple_of(place_in_first() * RX, RX), RX), :]
-
-
-def sum_kernel(got_ref, own_ref, out_ref, rest_ref):
-    i = place_in_first()
-    total = own_ref[...] - got_ref[i].astype(F32)
-    for j in range(RING):
+        out_ref[:, cols] = (home_ref[:, cols] + term).astype(BF16)
+
+
+def sum_kernel(got_ref, out_ref):
+    total = got_ref[0].astype(F32)
+    for j in range(1, RING):
         total += got_ref[j].astype(F32)
-    rounded = total.astype(BF16)
-    out_ref[0] = rounded
-    rest_ref[...] = total - rounded.astype(F32)
-
-
-def act_kernel(part_ref, rest_ref, out_ref):
-    total = rest_ref[...]
-    for i in range(RING):
+    out_ref[0] = total.astype(BF16)
+
+
+def act_kernel(part_ref, out_ref):
+    total = part_ref[0].astype(F32)
+    for i in range(1, RING):
         total += part_ref[i].astype(F32)
     gate, up, hg = total[:, :H], total[:, H : 2 * H], total[:, 2 * H :]
     sig = jax.nn.sigmoid(gate)
@@ -263,20 +258,13 @@
         **work,
     )(rows, held_down, wgu)
     held.append(held_down)
-    chip, own = call(
-        join_kernel,
-        (wide16, chunk32),
-        5,
-        limit_mb=16,
-        scratch_shapes=[pltpu.VMEM((ROWS, 3 * H), F32)],
-        **work,
-    )(home, other, *cross)
+    chip = call(join_kernel, wide16, 5, **work)(home, other, *cross)
     got = lax.all_to_all(
         chip.reshape(RING, RX, 3 * H), "dp", 0, 0, axis_index_groups=FIRST, tiled=True
     )
-    chunk, rest = call(sum_kernel, (chunk16, chunk32), 2)(got, own)
+    chunk = call(sum_kernel, chunk16, 1)(got)
     parts = lax.all_gather(chunk, "dp", axis=0, axis_index_groups=SECOND, tiled=True)
-    act = call(act_kernel, chunk16, 2)(parts, rest)
+    act = call(act_kernel, chunk16, 1)(parts)
     mine = lax.all_gather(act, "dp", axis=0, axis_index_groups=FIRST, tiled=True)
     mine = mine.reshape(ROWS, 3 * H)
     terms = call(other_kernel, pair16, 4, **work)(mine, *cross)

time: 98.4 us -> 98.6 us (level)
  no operation moved by 1% of the time
where the time goes in v7:
time: 98.6 us; the launch traced here: 98.2 us
  blocking collectives  63.1 us (64%)
  starting transfers between devices  25.1 us (25%)
  Pallas kernels  6.52 us (7%)
  waiting for transfers between devices  2.71 us (3%)
    all_gather x1, blocking collectives, local(): lax.all_gather(chunk, 'dp', axis=0, axis_index_groups=SECOND, tiled=True)  19.8 us
    all_to_all x1, blocking collectives, local(): lax.all_to_all(chip.reshape(RING, RX, 3 * H), 'dp', 0, 0, axis_index_grou...  14.9 us
    all_to_all x1, blocking collectives, local(): lax.all_to_all(back.reshape(E, PAIR, DW), 'expert', 0, 0, tiled=True)  14.6 us
    all_gather x1, blocking collectives, local(): lax.all_gather(act, 'dp', axis=0, axis_index_groups=FIRST, tiled=True)  13.8 us
    all_to_all x1, starting transfers between devices, local(): lax.all_to_all(send.reshape(E, PAIR, DW), 'expert', 0, 0, tiled=True)  11.8 us
    ppermute x3, starting transfers between devices, local(): cross = [lax.ppermute(w, 'dp', SWAP) for w in theirs]  6.24 us
    ppermute x1, starting transfers between devices, local(): got = lax.ppermute(terms, 'dp', SWAP)  5.13 us
    all_to_all x1, waiting for transfers between devices, local(): lax.all_to_all(send.reshape(E, PAIR, DW), 'expert', 0, 0, tiled=True)  2.23 us
  transfers between devices with their start and end apart: 6, of which 2 were waited for; matrix products, arithmetic and copies ran while one was open for 0% of the time, Pallas kernels for 2%

profile of v7, /device:TPU:8, one launch (start us, length us, event | category | flops | bytes accessed | tf_op | source)
XLA Modules:
  0.0 98.2 jit_solution(17527199428290404050)
XLA Ops:
  0.6 1.9 %shard_map.77 = (bf16[384,256]{1,0:T(8,128)(2,1)}, s32[64,2]{1,0:T(8,128)S(1)}, f32[64,2]{1,0:T(8,128)S(1)}, bf16[256,896]{1,0:T(8,128)(2,1)S(1)}, bf16[256,896]...) custom-call(s32[2,64]{1,0:T(2,128)} %bitcast.19, f32[2,64]{1,0:T(2,128)} %bitcast.20, ...), custom_call_target="tpu_custom_call" | custom-call | tf_op jit(solution)/shard_map/pallas_call | solution.py:238
  2.5 11.8 %all-to-all-start = ((bf16[16,24,256]{2,1,0:T(8,128)(2,1)}), bf16[16,24,256]{2,1,0:T(8,128)(2,1)S(1)}, u32[]{:S(2)}, u32[]{:S(2)}) async-start(bf16[16,24,256]{2,1,0:T(8,128)(2,1)} %bitcast.4), calls=%async_computation | async-start | bytes 393216 | tf_op jit(solution)/shard_map/all_to_all | solution.py:247
  14.3 1.9 %collective-permute-start.1 = (bf16[256,896]{1,0:T(8,128)(2,1)S(1)}, bf16[256,896]{1,0:T(8,128)(2,1)S(1)}, u32[]{:S(2)}, u32[]{:S(2)}) collective-permute-start(bf16[256,896]{1,0:T(8,128)(2,1)S(1)} %get-tuple-element.17), channel_id=1, source_target_pairs={{0,16},{16,0},{32,48},{48,32},{64,80},{80,64},{96,112},{112,96},{1... | collective-permute-start | bytes 1376264 | tf_op jit(solution)/shard_map/ppermute | solution.py:246
  16.2 2.4 %collective-permute-start.2 = (bf16[256,896]{1,0:T(8,128)(2,1)S(1)}, bf16[256,896]{1,0:T(8,128)(2,1)S(1)}, u32[]{:S(2)}, u32[]{:S(2)}) collective-permute-start(bf16[256,896]{1,0:T(8,128)(2,1)S(1)} %get-tuple-element.18), channel_id=1, source_target_pairs={{0,16},{16,0},{32,48},{48,32},{64,80},{80,64},{96,112},{112,96},{1... | collective-permute-start | bytes 1376264 | tf_op jit(solution)/shard_map/ppermute | solution.py:246
  18.6 1.9 %collective-permute-start.3 = (bf16[896,256]{1,0:T(8,128)(2,1)S(1)}, bf16[896,256]{1,0:T(8,128)(2,1)S(1)}, u32[]{:S(2)}, u32[]{:S(2)}) collective-permute-start(bf16[896,256]{1,0:T(8,128)(2,1)S(1)} %get-tuple-element.19), channel_id=1, source_target_pairs={{0,16},{16,0},{32,48},{48,32},{64,80},{80,64},{96,112},{112,96},{1... | collective-permute-start | bytes 1376264 | tf_op jit(solution)/shard_map/ppermute | solution.py:246
  20.6 2.2 %all-to-all-done = bf16[16,24,256]{2,1,0:T(8,128)(2,1)S(1)} async-done(((bf16[16,24,256]{2,1,0:T(8,128)(2,1)}), bf16[16,24,256]{2,1,0:T(8,128)(2,1)S(1)}, u32[]{:S(2)}, u32[]{:S(2)}) %all-to-all-start) | async-done | bytes 196640 | tf_op jit(solution)/shard_map/all_to_all | solution.py:247
  22.8 0.1 shard_map.78.rows_ref
  22.9 1.9 %collective-permute-start = (bf16[384,256]{1,0:T(8,128)(2,1)S(1)}, bf16[384,256]{1,0:T(8,128)(2,1)S(1)}, u32[]{:S(2)}, u32[]{:S(2)}) collective-permute-start(bf16[384,256]{1,0:T(8,128)(2,1)S(1)} %shard_map.78.rows_ref), channel_id=1, source_target_pairs={{0,16},{16,0},{32,48},{48,32},{64,80},{80,64},{96,112},{112,96},{1... | collective-permute-start | bytes 589832 | tf_op jit(solution)/shard_map/ppermute | solution.py:251
  24.8 1.7 %shard_map.79 = (f32[192,2688]{1,0:T(8,128)S(1)}, bf16[256,896]{1,0:T(8,128)(2,1)S(1)}, bf16[256,896]{1,0:T(8,128)(2,1)S(1)}) custom-call(bf16[384,256]{1,0:T(8,128)(2,1)S(1)} %shard_map.78.rows_ref, bf16[896,256]{1,0:T(8,128)(2,1)S(1)} %get-tuple-element.15.down_ref, bf16[256,3584]{1,0:T(8,128)(2,1)} %bitcast.17), custom_call_target="tpu_custom_call" | custom-call | flops 264241152 | bytes 4194304 | tf_op jit(solution)/shard_map/pallas_call | solution.py:252
  26.5 0.0 collective-permute-done.1.gate_ref
  26.5 0.0 collective-permute-done.rows_ref
  26.6 0.5 shard_map.80
  27.1 14.9 %all_to_all.15.got_ref = bf16[4,48,2688]{2,1,0:T(8,128)(2,1)S(1)} all-to-all(bf16[4,48,2688]{2,1,0:T(8,128)(2,1)S(1)} %bitcast.12), channel_id=1, replica_groups={{0,128,256,384},{32,160,288,416},{64,192,320,448},{96,224,352,480},{16,..., dimensions={0} | all-to-all | bytes 2064384 | tf_op jit(solution)/shard_map/all_to_all | solution.py:262
  42.0 0.1 shard_map.81
  42.1 19.8 %all_gather.6.part_ref = bf16[4,48,2688]{2,1,0:T(8,128)(2,1)S(1)} all-gather(bf16[1,48,2688]{2,1,0:T(8,128)(2,1)S(1)} %shard_map.81), channel_id=1, replica_groups={{0,32,64,96},{128,160,192,224},{256,288,320,352},{384,416,448,480},{16,..., dimensions={0}, use_global_device_ids=true | all-gather | bytes 1290240 | tf_op jit(solution)/shard_map/all_gather | solution.py:266
  61.9 0.2 shard_map.82
  62.2 13.8 %all_gather.7 = bf16[4,48,2688]{2,1,0:T(8,128)(2,1)S(1)} all-gather(bf16[1,48,2688]{2,1,0:T(8,128)(2,1)S(1)} %shard_map.82), channel_id=1, replica_groups={{0,128,256,384},{32,160,288,416},{64,192,320,448},{96,224,352,480},{16,..., dimensions={0}, use_global_device_ids=true | all-gather | bytes 1290240 | tf_op jit(solution)/shard_map/all_gather | solution.py:268
  76.0 0.6 shard_map.84
  76.5 5.1 %collective-permute-start.4 = (bf16[384,256]{1,0:T(8,128)(2,1)S(1)}, bf16[384,256]{1,0:T(8,128)(2,1)S(1)}, u32[]{:S(2)}, u32[]{:S(2)}) collective-permute-start(bf16[384,256]{1,0:T(8,128)(2,1)S(1)} %shard_map.84), channel_id=1, source_target_pairs={{0,16},{16,0},{32,48},{48,32},{64,80},{80,64},{96,112},{112,96},{1... | collective-permute-start | bytes 589832 | tf_op jit(solution)/shard_map/ppermute | solution.py:271
  81.7 0.6 shard_map.83
  82.2 0.5 collective-permute-done.4.got_ref
  82.7 0.1 shard_map.85
  82.8 14.6 %all_to_all.16 = bf16[16,24,256]{2,1,0:T(8,128)(2,1)S(1)} all-to-all(bf16[16,24,256]{2,1,0:T(8,128)(2,1)S(1)} %bitcast.15), channel_id=1, replica_groups=mesh['dp'=32,'expert'=16] {'expert'}, dimensions={0} | all-to-all | bytes 393216 | tf_op jit(solution)/shard_map/all_to_all | solution.py:276
  97.4 0.8 shard_map.86
  (2 shorter events, 0.0 us)
Async XLA Ops:
  2.5 20.3 %all-to-all-start = ((bf16[16,24,256]{2,1,0:T(8,128)(2,1)}), bf16[16,24,256]{2,1,0:T(8,128)(2,1)S(1)}, u32[]{:S(2)}, u32[]{:S(2)}) async-start(bf16[16,24,256]{2,1,0:T(8,128)(2,1)} %bitcast.4), calls=%async_computation | async-start | bytes 393216 | tf_op jit(solution)/shard_map/all_to_all | solution.py:247
  14.3 12.2 %collective-permute-start.1 = (bf16[256,896]{1,0:T(8,128)(2,1)S(1)}, bf16[256,896]{1,0:T(8,128)(2,1)S(1)}, u32[]{:S(2)}, u32[]{:S(2)}) collective-permute-start(bf16[256,896]{1,0:T(8,128)(2,1)S(1)} %get-tuple-element.17), channel_id=1, source_target_pairs={{0,16},{16,0},{32,48},{48,32},{64,80},{80,64},{96,112},{112,96},{1... | collective-permute-start | bytes 1376264 | tf_op jit(solution)/shard_map/ppermute | solution.py:246
  16.2 10.3 %collective-permute-start.2 = (bf16[256,896]{1,0:T(8,128)(2,1)S(1)}, bf16[256,896]{1,0:T(8,128)(2,1)S(1)}, u32[]{:S(2)}, u32[]{:S(2)}) collective-permute-start(bf16[256,896]{1,0:T(8,128)(2,1)S(1)} %get-tuple-element.18), channel_id=1, source_target_pairs={{0,16},{16,0},{32,48},{48,32},{64,80},{80,64},{96,112},{112,96},{1... | collective-permute-start | bytes 1376264 | tf_op jit(solution)/shard_map/ppermute | solution.py:246
  18.6 7.9 %collective-permute-start.3 = (bf16[896,256]{1,0:T(8,128)(2,1)S(1)}, bf16[896,256]{1,0:T(8,128)(2,1)S(1)}, u32[]{:S(2)}, u32[]{:S(2)}) collective-permute-start(bf16[896,256]{1,0:T(8,128)(2,1)S(1)} %get-tuple-element.19), channel_id=1, source_target_pairs={{0,16},{16,0},{32,48},{48,32},{64,80},{80,64},{96,112},{112,96},{1... | collective-permute-start | bytes 1376264 | tf_op jit(solution)/shard_map/ppermute | solution.py:246
  22.9 3.7 %collective-permute-start = (bf16[384,256]{1,0:T(8,128)(2,1)S(1)}, bf16[384,256]{1,0:T(8,128)(2,1)S(1)}, u32[]{:S(2)}, u32[]{:S(2)}) collective-permute-start(bf16[384,256]{1,0:T(8,128)(2,1)S(1)} %shard_map.78.rows_ref), channel_id=1, source_target_pairs={{0,16},{16,0},{32,48},{48,32},{64,80},{80,64},{96,112},{112,96},{1... | collective-permute-start | bytes 589832 | tf_op jit(solution)/shard_map/ppermute | solution.py:251
  76.5 6.2 %collective-permute-start.4 = (bf16[384,256]{1,0:T(8,128)(2,1)S(1)}, bf16[384,256]{1,0:T(8,128)(2,1)S(1)}, u32[]{:S(2)}, u32[]{:S(2)}) collective-permute-start(bf16[384,256]{1,0:T(8,128)(2,1)S(1)} %shard_map.84), channel_id=1, source_target_pairs={{0,16},{16,0},{32,48},{48,32},{64,80},{80,64},{96,112},{112,96},{1... | collective-permute-start | bytes 589832 | tf_op jit(solution)/shard_map/ppermute | solution.py:271
